TPU v7x, 128 devices: a whole 4x4x4 slice. The times are simulated.
128 devices in a mesh: lon: 16 (over y_hi, x, core), ch: 8 (over y_lo, z).
Axes of the slice: x: 4, y: 4 (y_hi: 2, y_lo: 2; y = y_hi * 2 + y_lo), z: 4, core: 2. Of those that a mesh axis runs over, the one named last changes fastest.
Arguments:
- latents: bfloat16 [96, 2, 1024, 640], P(None, None, 'lon', 'ch'), may hold values from -11 to 11
- next_latents: bfloat16 [96, 2, 1024, 640], P('ch', None, 'lon'), may hold values from -18 to 18
- timesteps: int32 [2], replicated, may hold values from 400 to 900
- resume_steps: int32 [2], replicated, may hold values from 40 to 100
- conv_weights: bfloat16 [2, 3, 3, 640, 640], replicated, may hold values from -0.078125 to 0.078125
- conv_bias: float32 [2, 640], replicated, may hold values from -1.5 to 1.5
- norm_gain: float32 [2, 640], replicated, may hold values from 0.1 to 1.9
- norm_shift: float32 [2, 640], replicated, may hold values from -1.5 to 1.5
- time_w1: float32 [320, 1280], replicated, may hold values from -0.3125 to 0.3125
- time_w2: float32 [1280, 640], replicated, may hold values from -0.15625 to 0.15625
Outputs:
- predicted_noise: bfloat16 [96, 2, 1024, 640], P('ch', None, 'lon')
- logprob: float32 [2], replicated
All inputs are finite; a program needn't handle non-finite values.
Results may differ from a plain program's by a relative error of at most 0.0044.
Values may be sent and summed in bfloat16 or wider, within the bound.
No kernel may reach another device: no remote copies, remote signals or barrier semaphores. Data moves between devices by JAX's collectives and lax.ppermute only.
A program may use at most 576 MiB of HBM per device.

v0:
```python
import functools
import math

import jax
import jax.numpy as jnp
import numpy as np
from jax import lax
from jax.experimental import pallas as pl
from jax.experimental.pallas import tpu as pltpu
from jax.sharding import PartitionSpec as P

GROUPS = 32
C = 640
LAT = 96
ROWS = 12
COLS = 64
SRC = 8
PART = C // SRC
WIDTH = C // GROUPS
TAPS = 9
F32 = jnp.float32
BF16 = jnp.bfloat16
VMEM = pl.BlockSpec(memory_space=pltpu.VMEM)
SMEM = pl.BlockSpec(memory_space=pltpu.SMEM)
ANY = pl.BlockSpec(memory_space=pl.ANY)
CHUNK = 16
LIMIT = 32 * 2**20


def roll(x, by):
    by %= 128
    return x if by == 0 else pltpu.roll(x, by, 1)


def side_lanes(of_left, of_right):
    out = np.zeros((128, 1024), np.float32)
    for q in range(-1, 7):
        at = 128 * (q + 1)
        out[of_left(q), at] = 1
        out[of_left(q + 6), at + 64] = 1
        out[of_right(q), at + 63] = 1
        out[of_right(q + 6), at + 127] = 1
    return out.astype(BF16)


def halo_lane(s, side, row):
    return 32 * s + 16 * side + row + 1


def halo_taps():
    out = np.zeros((256, TAPS * 128), np.float32)
    for i in range(3):
        for k in range(3):
            for s in range(2):
                for side in range(2):
                    for row in range(-1, 13):
                        source = 128 * s + 16 * (3 * side + k) + row + i - 1 + 2
                        out[source, 128 * (3 * i + k) + halo_lane(s, side, row)] = 1
    return out.astype(BF16)


def lanes(rows):
    return lax.broadcasted_iota(jnp.int32, (rows, 128), 1)


def members(rows, first, base):
    chan = lax.broadcasted_iota(jnp.int32, (rows, 128), 0) + first
    low = (lanes(rows) - base) * WIDTH
    return (chan >= low) & (chan < low + WIDTH)


def silu(x):
    return 0.5 * x * (1.0 + jnp.tanh(0.5 * x))


def pack_kernel(s, part_ref, main_ref, *rest):
    if s == 1:
        prev_ref, *rest = rest
    pay_ref, sums_ref, taken, turned = rest
    e = pl.program_id(0)
    x = main_ref[0].astype(F32)

    @pl.when(e == 0)
    def _():
        taken[...] = jnp.zeros_like(taken)
        turned[...] = jnp.zeros_like(turned)
        sums_ref[...] = jnp.zeros_like(sums_ref) if s == 0 else prev_ref[...]

    row = sums_ref[...]
    for k in range(2):
        column = jnp.sum(jnp.sum(x * x if k else x, axis=0), axis=1, keepdims=True)
        own = members(CHUNK, part_ref[0] * PART + e * CHUNK, 64 * k + 32 * s)
        row += jnp.sum(jnp.where(own, column, 0.0), axis=0, keepdims=True)
    sums_ref[...] = row

    taken[:, 0:LAT] = x.reshape(COLS * CHUNK, LAT)
    for j in range(CHUNK):
        plain = taken[pl.ds(j, COLS, stride=CHUNK), :]
        both = jnp.concatenate([plain, roll(plain, -6)], axis=0).T
        turned[pl.ds(CHUNK + j, LAT, stride=CHUNK), :] = both[0:LAT, :]

    low = lanes(CHUNK) < 64

    def tile(r):
        return turned[CHUNK * (r + 1) : CHUNK * (r + 2), :]

    for d in range(SRC):
        for q in range(6):
            pay_ref[d, q] = tile(d * ROWS + q).astype(BF16)
        edge = jnp.where(low, tile(d * ROWS - 1), tile(d * ROWS + 6))
        pay_ref[d, 6] = edge.astype(BF16)


def pack(s, part, latents, before):
    line = pl.BlockSpec((1, 128), lambda e: (0, 0))
    return pl.pallas_call(
        functools.partial(pack_kernel, s),
        grid=(PART // CHUNK,),
        in_specs=[SMEM, pl.BlockSpec((1, COLS, CHUNK, LAT), lambda e: (s, 0, e, 0))]
        + [line] * len(before),
        out_specs=[pl.BlockSpec((SRC, 7, CHUNK, 128), lambda e: (0, 0, e, 0)), line],
        out_shape=[
            jax.ShapeDtypeStruct((SRC, 8, PART, 128), BF16),
            jax.ShapeDtypeStruct((1, 128), F32),
        ],
        scratch_shapes=[
            pltpu.VMEM((COLS * CHUNK, 128), F32),
            pltpu.VMEM(((LAT + 8) * CHUNK, 128), F32),
        ],
        compiler_params=pltpu.CompilerParams(vmem_limit_bytes=LIMIT),
        name=f"pack_latents_{s}",
    )(part, latents, *before)


def halo_kernel(left_ref, first_ref, last_ref, right_ref, _, pay_ref):
    lane = lanes(PART)
    pad = jnp.zeros((PART, 128 - LAT), F32)
    near = [left_ref[0, 0], left_ref[0, 1], first_ref[0, 0], last_ref[0, 0],
            right_ref[0, 0], right_ref[0, 1]]
    near = [jnp.concatenate([col.astype(F32), pad], axis=1) for col in near]
    for d in range(SRC):
        halo = jnp.zeros((PART, 128), F32)
        for kind in range(6):
            own = (lane >= 16 * kind) & (lane < 16 * kind + 16)
            halo = jnp.where(own, roll(near[kind], 16 * kind + 2 - d * ROWS), halo)
        pay_ref[d, 0] = halo.astype(BF16)


def pack_halo(s, latents, left, right, pay):
    pair = (1, 2, PART, LAT)
    one = (1, 1, PART, LAT)
    return pl.pallas_call(
        halo_kernel,
        grid=(1,),
        in_specs=[
            pl.BlockSpec(pair, lambda e: (s, 0, 0, 0)),
            pl.BlockSpec(one, lambda e: (s, 0, 0, 0)),
            pl.BlockSpec(one, lambda e: (s, COLS - 1, 0, 0)),
            pl.BlockSpec(pair, lambda e: (s, 0, 0, 0)),
            ANY,
        ],
        out_specs=pl.BlockSpec((SRC, 1, PART, 128), lambda e: (0, 7, 0, 0)),
        out_shape=jax.ShapeDtypeStruct((SRC, 8, PART, 128), BF16),
        input_output_aliases={4: 0},
        compiler_params=pltpu.CompilerParams(vmem_limit_bytes=LIMIT),
        name=f"pack_halo_{s}",
    )(left, latents, latents, right, pay)


def weight_kernel(w_ref, o_ref):
    at = pl.multiple_of(pl.program_id(0) * C, 128)
    o_ref[:, pl.ds(at, C)] = w_ref[0, 0].T


def turn_weights(j, weights):
    taps = weights.reshape(2, TAPS, C, C)
    return pl.pallas_call(
        weight_kernel,
        grid=(TAPS,),
        in_specs=[pl.BlockSpec((1, 1, C, C), lambda t: (j, t, 0, 0))],
        out_specs=VMEM,
        out_shape=pltpu.VMEM((C, TAPS * C), BF16),
        compiler_params=pltpu.CompilerParams(vmem_limit_bytes=LIMIT),
        cost_estimate=pl.CostEstimate(
            flops=TAPS * 2 * C * C * 256, bytes_accessed=15_000_000, transcendentals=0
        ),
        name=f"turn_weights_{j}",
    )(taps)


def target_kernel(upper_ref, lower_ref, o_ref):
    o_ref[0, 0] = jnp.concatenate([upper_ref[0, 0], lower_ref[0, 0]], axis=0).T


def turn_target(target):
    block = (1, 1, COLS, C)
    return pl.pallas_call(
        target_kernel,
        grid=(2, 6),
        in_specs=[
            pl.BlockSpec(block, lambda s, q: (q, s, 0, 0)),
            pl.BlockSpec(block, lambda s, q: (q + 6, s, 0, 0)),
        ],
        out_specs=pl.BlockSpec((1, 1, C, 128), lambda s, q: (s, q, 0, 0)),
        out_shape=jax.ShapeDtypeStruct((2, 6, C, 128), BF16),
        compiler_params=pltpu.CompilerParams(vmem_limit_bytes=LIMIT),
        name="turn_target",
    )(target, target)


def in_vmem(x):
    return pltpu.with_memory_space_constraint(x, pltpu.VMEM)


def affine(sums_ref, par_ref, s, j, scale, offset):
    count = float(LAT * 1024 * WIDTH)
    row = jnp.sum(sums_ref[...], axis=0, keepdims=True)

    def of_channel(base):
        picked = jnp.where(members(C, 0, base), row, 0.0)
        return jnp.sum(picked, axis=1, keepdims=True) / count

    mean = of_channel(32 * s)
    spread = of_channel(64 + 32 * s) - mean * mean
    factor = lax.rsqrt(spread + 1e-05) * par_ref[:, 2 * j : 2 * j + 1]
    rest = par_ref[:, 2 * j + 1 : 2 * j + 2] - mean * factor
    scale[...] = jnp.broadcast_to(factor, scale.shape)
    offset[...] = jnp.broadcast_to(rest, offset.shape)


def spread_taps(xs, at, rows, tiles, edge, sides, part):
    lane = lanes(rows)
    low = lane < 64
    first = (lane == 0) | (lane == 64)
    last = (lane == 63) | (lane == 127)
    for q in range(-1, 7):
        if q == -1:
            tile = jnp.where(low, edge, roll(tiles[5], 64))
        elif q == 6:
            tile = jnp.where(low, roll(tiles[0], 64), edge)
        else:
            tile = tiles[q]
        side = sides[pl.ds(at, rows), 128 * (q + 1) : 128 * (q + 2)]
        taps = (jnp.where(first, side, roll(tile, 1)), tile, jnp.where(last, side, roll(tile, -1)))
        for k, tap in enumerate(taps):
            if q == -1:
                tap = jnp.where(low & (part == 0), 0.0, tap)
            elif q == 6:
                tap = jnp.where((~low) & (part == SRC - 1), 0.0, tap)
            xs[pl.ds(k * C + at, rows), 128 * (q + 1) : 128 * (q + 2)] = tap.astype(BF16)


def product(wv, xs, n):
    x = jnp.concatenate([xs[:, n + 128 * i : n + 128 * i + 256] for i in range(3)], axis=0)
    return jnp.dot(wv[...], x, preferred_element_type=F32)


def first_kernel(
    s, part_ref, sums_ref, par_ref, pick_ref, recv_hbm, wv, *rest,
):
    if s == 1:
        taps_ref, recv_other, before_sums, before_next, before_prev, *rest = rest
        hid, out_sums, to_next, to_prev, out_halo, *rest = rest
        xs, scale, offset, recv, sides, sems, other, xh = rest
    else:
        hid, out_sums, to_next, to_prev, *rest = rest
        xs, scale, offset, recv, sides, sems = rest
    fetch = pltpu.make_async_copy(recv_hbm, recv, sems.at[0])
    fetch.start()
    if s == 1:
        fetch_other = pltpu.make_async_copy(recv_other.at[:, 7], other, sems.at[1])
        fetch_other.start()
    part = part_ref[0]

    def act(x, a, o):
        return silu(x.astype(F32) * a + o)

    def halo_act(x):
        r = (lanes(C) & 15) - 2
        outside = ((part == 0) & (r < 0)) | ((part == SRC - 1) & (r >= ROWS))
        return jnp.where(outside, 0.0, act(x, scale[...], offset[...])).astype(BF16)

    if s == 1:
        affine(sums_ref, par_ref, 0, 0, scale, offset)
        fetch_other.wait()
        halo_other = halo_act(other[...].reshape(C, 128))
    affine(sums_ref, par_ref, s, 0, scale, offset)
    fetch.wait()
    halo = halo_act(recv[:, 7].reshape(C, 128))
    sides[...] = jnp.dot(halo, pick_ref[...], preferred_element_type=F32)
    if s == 1:
        both = jnp.concatenate([halo_other, halo], axis=1)
        for t in range(TAPS):
            picked = jnp.dot(both, taps_ref[:, 128 * t : 128 * t + 128], preferred_element_type=F32)
            xh[C * t : C * (t + 1), :] = picked.astype(BF16)

    @pl.loop(0, SRC)
    def _(b):
        at = pl.multiple_of(b * PART, PART)
        a, o = scale[pl.ds(at, PART), :], offset[pl.ds(at, PART), :]
        tiles = [act(recv[b, q], a, o) for q in range(7)]
        spread_taps(xs, at, PART, tiles[:6], tiles[6], sides, part)

    bias = par_ref[:, 5 + s : 6 + s]
    for n in range(0, 768, 256):
        hid[:, n : n + 256] = product(wv, xs, n) + bias
    if s == 1:
        halo = jnp.dot(wv[...], xh[...], preferred_element_type=F32)
        bias = jnp.where(lanes(C) < 32, par_ref[:, 5:6], par_ref[:, 6:7])
        out_halo[...] = (halo + bias).astype(BF16)

    row = jnp.zeros((1, 128), F32) if s == 0 else before_sums[0:1, :]
    for at in range(0, C, 128):
        pieces = [hid[at : at + 128, 128 * q : 128 * (q + 1)] for q in range(6)]
        for k in range(2):
            column = jnp.sum(sum(p * p if k else p for p in pieces), axis=1, keepdims=True)
            own = members(128, at, 64 * k + 32 * s)
            row += jnp.sum(jnp.where(own, column, 0.0), axis=0, keepdims=True)
        if s == 0:
            after, ahead = roll(pieces[5], 64), pieces[0]
        else:
            low = lanes(128) < 64
            after = jnp.where(low, before_next[at : at + 128, :].astype(F32), pieces[5])
            ahead = jnp.where(low, before_prev[at : at + 128, :].astype(F32), roll(pieces[0], 64))
        to_next[at : at + 128, :] = after.astype(BF16)
        to_prev[at : at + 128, :] = ahead.astype(BF16)
    out_sums[...] = jnp.broadcast_to(row, out_sums.shape)


def first_conv(s, part, sums, params, pick, recv, weights, before):
    tile = jax.ShapeDtypeStruct((C, 128), BF16)
    more = [VMEM, ANY, VMEM, VMEM, VMEM] if s == 1 else []
    return pl.pallas_call(
        functools.partial(first_kernel, s),
        in_specs=[SMEM, VMEM, VMEM, VMEM, ANY, VMEM] + more,
        out_specs=[VMEM] * (4 + s),
        out_shape=[
            pltpu.VMEM((C, 768), F32),
            jax.ShapeDtypeStruct((128, 128), F32),
        ]
        + [tile] * (2 + s),
        scratch_shapes=[
            pltpu.VMEM((3 * C, 1024), BF16),
            pltpu.VMEM((C, 128), F32),
            pltpu.VMEM((C, 128), F32),
            pltpu.VMEM((SRC, 8, PART, 128), BF16),
            pltpu.VMEM((C, 1024), F32),
            pltpu.SemaphoreType.DMA((2,)),
        ]
        + [pltpu.VMEM((SRC, PART, 128), BF16), pltpu.VMEM((TAPS * C, 128), BF16)][: 2 * s],
        compiler_params=pltpu.CompilerParams(vmem_limit_bytes=LIMIT),
        cost_estimate=pl.CostEstimate(
            flops=2 * 768 * C * C * 9, bytes_accessed=12_000_000, transcendentals=0
        ),
        name=f"first_conv_{s}",
    )(part, sums, params, pick, recv, in_vmem(weights), *before)


def second_kernel(
    part_ref, coef_ref, sums_ref, par_ref, pick_ref, near_ref, prev_ref, next_ref,
    hid0, hid1, wv, recv0, recv1, target_hbm,
    noise_hbm, out_ref,
    xs, lat, target, noise_out, sides, scale, offset, sems,
):
    copies = [
        pltpu.make_async_copy(recv0.at[:, 0:6], lat.at[0], sems.at[0]),
        pltpu.make_async_copy(target_hbm.at[0], target.at[0], sems.at[1]),
        pltpu.make_async_copy(recv1.at[:, 0:6], lat.at[1], sems.at[2]),
        pltpu.make_async_copy(target_hbm.at[1], target.at[1], sems.at[3]),
    ]
    for copy in copies:
        copy.start()
    part = part_ref[0]
    result = jnp.zeros((1, 128), F32)
    stores = []
    for s in range(2):
        hid = (hid0, hid1)[s]
        affine(sums_ref, par_ref, s, 1, scale, offset)
        halo = silu(near_ref[...].astype(F32) * scale[...] + offset[...]).astype(BF16)
        sides[...] = jnp.dot(halo, pick_ref[s], preferred_element_type=F32)

        @pl.loop(0, SRC)
        def _(b):
            at = pl.multiple_of(b * PART, PART)
            rows = pl.ds(at, PART)
            a, o = scale[rows, :], offset[rows, :]
            low = lanes(PART) < 64

            def act(x):
                return silu(x * a + o)

            tiles = [act(hid[rows, 128 * q : 128 * (q + 1)]) for q in range(6)]
            above, below = prev_ref[rows, :].astype(F32), next_ref[rows, :].astype(F32)
            if s == 0:
                edge = jnp.where(low, above, roll(below, 64))
            else:
                edge = jnp.where(low, roll(above, 64), below)
            spread_taps(xs, at, PART, tiles, act(edge), sides, part)

        copies[2 * s].wait()
        copies[2 * s + 1].wait()
        bias = par_ref[:, 4:5]
        keep, gain = coef_ref[2 * s], coef_ref[2 * s + 1]
        acc = jnp.zeros((8, 128), F32)
        for n in range(0, 768, 256):
            out = product(wv, xs, n) + bias
            for h in range(2):
                q = n // 128 + h
                mine = lat[s, :, q].reshape(C, 128).astype(F32)
                noise = (out[:, 128 * h : 128 * h + 128] + mine).astype(BF16)
                center = keep * mine + gain * noise.astype(F32)
                diff = target[s, q].astype(F32) - center
                acc += jnp.sum((diff * diff).reshape(C // 8, 8, 128), axis=0)
                plain = noise.T
                noise_out[s, q] = plain[0:64]
                noise_out[s, q + 6] = plain[64:128]
        store = pltpu.make_async_copy(noise_out.at[s], noise_hbm.at[:, s], sems.at[4 + s])
        store.start()
        stores.append(store)
        value = jnp.sum(acc, axis=(0, 1), keepdims=True)
        result = jnp.where(lanes(1) == s, value, result)
    out_ref[...] = jnp.broadcast_to(result, out_ref.shape)
    for store in stores:
        store.wait()


def second_conv(part, coef, sums, params, pick, tiles, hidden, weights, recv, target):
    return pl.pallas_call(
        second_kernel,
        in_specs=[SMEM, SMEM] + [VMEM] * 9 + [ANY] * 3,
        out_specs=[ANY, VMEM],
        out_shape=[
            jax.ShapeDtypeStruct((ROWS, 2, COLS, C), BF16),
            jax.ShapeDtypeStruct((128, 128), F32),
        ],
        scratch_shapes=[
            pltpu.VMEM((3 * C, 1024), BF16),
            pltpu.VMEM((2, SRC, 6, PART, 128), BF16),
            pltpu.VMEM((2, 6, C, 128), BF16),
            pltpu.VMEM((2, ROWS, COLS, C), BF16),
            pltpu.VMEM((C, 1024), F32),
            pltpu.VMEM((C, 128), F32),
            pltpu.VMEM((C, 128), F32),
            pltpu.SemaphoreType.DMA((6,)),
        ],
        compiler_params=pltpu.CompilerParams(vmem_limit_bytes=LIMIT),
        cost_estimate=pl.CostEstimate(
            flops=4 * 768 * C * C * 9, bytes_accessed=20_000_000, transcendentals=0
        ),
        name="second_conv",
    )(
        part, coef, sums, params, pick, *tiles, *[in_vmem(h) for h in hidden],
        in_vmem(weights), *recv, target,
    )


def time_embed(timesteps, time_w1, time_w2):
    half = time_w1.shape[0] // 2
    freqs = jnp.exp(-math.log(10000.0) * jnp.arange(half, dtype=F32) / half)
    angles = timesteps.astype(F32)[:, None] * freqs[None, :]
    features = jnp.concatenate([jnp.cos(angles), jnp.sin(angles)], axis=1)
    hidden = jax.nn.silu(jnp.dot(features, time_w1, precision=lax.Precision.HIGHEST))
    return jnp.dot(hidden, time_w2, precision=lax.Precision.HIGHEST)


def plan(steps):
    frac = steps.astype(F32) / 1000.0
    return jnp.cos((frac + 0.008) / 1.008 * (math.pi / 2.0)) ** 2


def everywhere(rows):
    got = lax.all_to_all(rows.reshape(128, 1, 128), ("lon", "ch"), 0, 0, tiled=True)
    return got.reshape(128, 128)


def ring(axis, step, wrap):
    size = lax.axis_size(axis)
    return [(i, (i + step) % size) for i in range(size) if wrap or 0 <= i + step < size]


def swap(array, axis):
    return lax.all_to_all(array, axis, split_axis=0, concat_axis=0, tiled=True)


def after(value, *others):
    return lax.optimization_barrier((value,) + others)[0]


def butterfly(x):
    for axis in ("lon", "ch"):
        step = 1
        while step < lax.axis_size(axis):
            pairs = [(i, i ^ step) for i in range(lax.axis_size(axis))]
            x = x + lax.ppermute(x, axis, pairs)
            step *= 2
    return x


def body(
    latents, next_latents, timesteps, resume_steps, conv_weights, conv_bias,
    norm_gain, norm_shift, time_w1, time_w2,
):
    part = lax.axis_index("ch").astype(jnp.int32).reshape(1)
    first_pick = jnp.asarray(side_lanes(lambda r: 16 + r + 2, lambda r: 64 + r + 2))
    second_pick = jnp.asarray(
        np.stack(
            [
                side_lanes(lambda r: halo_lane(s, 0, r), lambda r: halo_lane(s, 1, r))
                for s in range(2)
            ]
        )
    )
    tap_pick = jnp.asarray(halo_taps())

    cells = latents.transpose(1, 2, 3, 0)
    left = lax.ppermute(cells[:, COLS - 2 :], "lon", ring("lon", 1, True))
    right = lax.ppermute(cells[:, :2], "lon", ring("lon", -1, True))
    pay0, sums = pack(0, part, cells, ())
    pay0 = pack_halo(0, cells, left, right, pay0)
    recv0 = swap(pay0, "ch")
    pay1, sums = pack(1, part, after(cells, pay0), (sums,))
    pay1 = pack_halo(1, cells, left, right, pay1)
    conv_weights, time_w1, following = after((conv_weights, time_w1, next_latents), sums)
    sums = butterfly(sums)
    recv1 = swap(after(pay1, recv0), "ch")
    turned = [turn_weights(j, conv_weights) for j in range(2)]
    target = turn_target(following)

    temb = time_embed(timesteps, time_w1, time_w2)
    columns = [
        norm_gain[0], norm_shift[0], norm_gain[1], norm_shift[1], conv_bias[1],
        conv_bias[0] + temb[0], conv_bias[0] + temb[1],
    ]
    params = jnp.pad(jnp.stack(columns, axis=1), ((0, 0), (0, 128 - len(columns))))

    alpha = plan(timesteps)
    prior = plan(timesteps - resume_steps)
    variance = (1.0 - prior) / (1.0 - alpha) * (1.0 - alpha / prior)
    keep = (1.0 - prior) * jnp.sqrt(alpha / (prior * (1.0 - alpha)))
    ratio = jnp.sqrt(prior) / jnp.sqrt(alpha)
    coef = jnp.stack([ratio, keep - ratio * jnp.sqrt(1.0 - alpha)], axis=1).reshape(4)

    hid0, *before = first_conv(0, part, sums, params, first_pick, recv0, turned[0], ())
    hid1, sums, to_next, to_prev, near = first_conv(
        1, part, sums, params, first_pick, recv1, turned[0], (tap_pick, recv0, *before)
    )
    from_prev = lax.ppermute(to_next, "ch", ring("ch", 1, False))
    from_next = lax.ppermute(to_prev, "ch", ring("ch", -1, False))
    sums = everywhere(sums)
    noise, terms = second_conv(
        part, coef, sums, params, second_pick, (near, from_prev, from_next),
        (hid0, hid1), turned[1], (recv0, recv1), target,
    )
    squares = jnp.sum(everywhere(terms), axis=0)[:2]
    logprob = (
        -squares / (2.0 * variance) / float(LAT * 1024 * C)
        - 0.5 * jnp.log(variance)
        - 0.5 * math.log(2.0 * math.pi)
    )
    return (noise, logprob)


def solution(mesh):
    return jax.shard_map(
        body,
        mesh=mesh,
        in_specs=(
            P(None, None, "lon", "ch"),
            P("ch", None, "lon", None),
            P(), P(), P(), P(), P(), P(), P(), P(),
        ),
        out_specs=(P("ch", None, "lon", None), P()),
        check_vma=False,
    )
```

profile of v0, /device:TPU:1, one launch (start us, length us, event | category | flops | bytes accessed | tf_op | source)
XLA Modules:
  0.0 210.6 jit_solution(17335277670109471343)
XLA Ops:
  0.6 1.7 fusion.14
  2.4 1.4 collective-permute-start.1
  3.8 1.2 collective-permute-start
  5.0 0.8 fusion.11
  6.4 1.7 copy-done.1
  8.2 3.7 %pack_latents_0.1 = (bf16[8,8,80,128]{3,2,1,0:T(8,128)(2,1)S(1)}, f32[1,128]{1,0:T(1,128)S(1)}) custom-call(s32[1]{0:T(128)} %bitcast.part_ref, bf16[2,64,80,96]{3,2,1,0:T(8,128)(2,1)S(1)} %bitcast.31), custom_call_target="tpu_custom_call" | custom-call | tf_op jit(solution)/shard_map/pack_latents_0/pallas_call | solution.py:116
  12.3 1.1 copy-done.16
  13.4 6.2 %all-to-all-start = ((bf16[8,8,80,128]{3,2,1,0:T(8,128)(2,1)}), bf16[8,8,80,128]{3,2,1,0:T(8,128)(2,1)}, u32[]{:S(2)}, u32[]{:S(2)}) async-start(bf16[8,8,80,128]{3,2,1,0:T(8,128)(2,1)} %copy-done.16), calls=%async_computation | async-start | bytes 2621440 | tf_op jit(solution)/shard_map/all_to_all | solution.py:482
  19.8 1.7 copy-done.3
  21.5 3.7 %pack_latents_1.1 = (bf16[8,8,80,128]{3,2,1,0:T(8,128)(2,1)S(1)}, f32[1,128]{1,0:T(1,128)S(1)}) custom-call(s32[1]{0:T(128)} %bitcast.part_ref, bf16[2,64,80,96]{3,2,1,0:T(8,128)(2,1)S(1)} %bitcast.34, f32[1,128]{1,0:T(1,128)S(1)} %get-tuple-element.24.rest_0_), custom_call_target="tpu_custom_call" | custom-call | tf_op jit(solution)/shard_map/pack_latents_1/pallas_call | solution.py:116
  25.2 1.0 copy-done.13
  26.3 3.6 %collective-permute-start.2 = (f32[1,128]{1,0:T(1,128)S(1)}, f32[1,128]{1,0:T(1,128)S(1)}, u32[]{:S(2)}, u32[]{:S(2)}) collective-permute-start(f32[1,128]{1,0:T(1,128)S(1)} %get-tuple-element.25), channel_id=1, source_target_pairs={{0,8},{8,0},{16,24},{24,16},{32,40},{40,32},{48,56},{56,48},{64,72... | collective-permute-start | bytes 1544 | tf_op jit(solution)/shard_map/ppermute | solution.py:494
  30.0 0.7 collective-permute-done.2
  30.9 2.6 %collective-permute-done.3 = f32[1,128]{1,0:T(1,128)S(1)} collective-permute-done((f32[1,128]{1,0:T(1,128)S(1)}, f32[1,128]{1,0:T(1,128)S(1)}, u32[]{:S(2)}, u32[]{:S(2)}) %collective-permute-start.3) | collective-permute-done | bytes 544 | tf_op jit(solution)/shard_map/ppermute | solution.py:494
  33.5 2.5 %collective-permute-start.4 = (f32[1,128]{1,0:T(1,128)S(1)}, f32[1,128]{1,0:T(1,128)S(1)}, u32[]{:S(2)}, u32[]{:S(2)}) collective-permute-start(f32[1,128]{1,0:T(1,128)S(1)} %add.63), channel_id=1, source_target_pairs={{0,32},{8,40},{16,48},{24,56},{32,0},{40,8},{48,16},{56,24},{64,96... | collective-permute-start | bytes 1544 | tf_op jit(solution)/shard_map/ppermute | solution.py:494
  36.0 2.3 %fusion.5 = f32[2,1280]{1,0:T(2,128)S(1)} fusion(f32[320,1280]{1,0:T(8,128)} %param.21, f32[2,160]{1,0:T(2,128)S(1)} %get-tuple-element.54, f32[2,160]{1,0:T(2,128)S(1)} %get-tuple-element.53), kind=kOutput, calls=%fused_computation.6 | convolution fusion | flops 9831040 | bytes 1651200 | tf_op jit(solution)/shard_map/dot_general | solution.py:462
  38.3 1.7 copy-done.4
  40.4 1.1 copy-done.15
  41.5 2.6 %collective-permute-start.5 = (f32[1,128]{1,0:T(1,128)S(1)}, f32[1,128]{1,0:T(1,128)S(1)}, u32[]{:S(2)}, u32[]{:S(2)}) collective-permute-start(f32[1,128]{1,0:T(1,128)S(1)} %add.64), channel_id=1, source_target_pairs={{0,64},{8,72},{16,80},{24,88},{32,96},{40,104},{48,112},{56,120},{... | collective-permute-start | bytes 1544 | tf_op jit(solution)/shard_map/ppermute | solution.py:494
  44.1 4.5 %all-to-all-start.1 = ((bf16[8,8,80,128]{3,2,1,0:T(8,128)(2,1)}), bf16[8,8,80,128]{3,2,1,0:T(8,128)(2,1)}, u32[]{:S(2)}, u32[]{:S(2)}) async-start(bf16[8,8,80,128]{3,2,1,0:T(8,128)(2,1)} %copy-done.15), calls=%async_computation.1 | async-start | bytes 2621440 | tf_op jit(solution)/shard_map/all_to_all | solution.py:482
  48.7 1.7 fusion
  50.4 1.5 collective-permute-start.6
  52.5 12.1 %collective-permute-done.6 = f32[1,128]{1,0:T(1,128)S(1)} collective-permute-done((f32[1,128]{1,0:T(1,128)S(1)}, f32[1,128]{1,0:T(1,128)S(1)}, u32[]{:S(2)}, u32[]{:S(2)}) %collective-permute-start.6) | collective-permute-done | bytes 544 | tf_op jit(solution)/shard_map/ppermute | solution.py:494
  64.7 2.4 %collective-permute-start.7 = (f32[1,128]{1,0:T(1,128)S(1)}, f32[1,128]{1,0:T(1,128)S(1)}, u32[]{:S(2)}, u32[]{:S(2)}) collective-permute-start(f32[1,128]{1,0:T(1,128)S(1)} %add.66), channel_id=1, source_target_pairs={{0,2},{1,3},{2,0},{3,1},{4,6},{5,7},{6,4},{7,5},{8,10},{9,11},{10,... | collective-permute-start | bytes 1544 | tf_op jit(solution)/shard_map/ppermute | solution.py:494
  67.1 5.2 %copy-done.5 = bf16[2,3,3,640,640]{4,3,2,1,0:T(8,128)(2,1)S(1)} copy-done((bf16[2,3,3,640,640]{4,3,2,1,0:T(8,128)(2,1)S(1)}, bf16[2,3,3,640,640]{4,3,2,1,0:T(8,128)(2,1)}, u32[]{:S(2)}) %copy-start.5) | copy-done | bytes 14745624
  72.2 2.5 %turn_weights_0.1.wv = bf16[640,5760]{1,0:T(8,128)(2,1)S(1)} custom-call(bf16[2,9,640,640]{3,2,1,0:T(8,128)(2,1)S(1)} %bitcast.37), custom_call_target="tpu_custom_call" | custom-call | flops 1887436800 | bytes 15000000 | tf_op jit(solution)/shard_map/turn_weights_0/pallas_call | solution.py:177
  74.8 2.9 %copy-done.8 = bf16[640,5760]{1,0:T(8,128)(2,1)} copy-done((bf16[640,5760]{1,0:T(8,128)(2,1)}, bf16[640,5760]{1,0:T(8,128)(2,1)S(1)}, u32[]{:S(2)}) %copy-start.8) | copy-done | bytes 7372824
  78.3 1.8 collective-permute-start.8
  80.0 1.3 stack.17
  81.4 1.6 copy.27
  83.0 1.0 pad.4.par_ref
  84.7 3.1 %copy-done.9 = bf16[640,5760]{1,0:T(8,128)(2,1)S(1)} copy-done((bf16[640,5760]{1,0:T(8,128)(2,1)S(1)}, bf16[640,5760]{1,0:T(8,128)(2,1)}, u32[]{:S(2)}) %copy-start.9) | copy-done | bytes 7372824
  87.8 12.0 %first_conv_0.1 = (f32[640,768]{1,0:T(8,128)S(1)}, f32[128,128]{1,0:T(8,128)S(1)}, bf16[640,128]{1,0:T(8,128)(2,1)S(1)}, bf16[640,128]{1,0:T(8,128)(2,1)S(1)}) custom-call(s32[1]{0:T(128)} %bitcast.part_ref, f32[1,128]{1,0:T(1,128)S(1)} %add.68.sums_ref, f32[640,128]{1,0:T(8,128)S(1)} %pad.4.par_ref, bf16[128,1024]{1,0:T(8,128)(2,1)S(1)} %copy-done.25, ...), custom_call_target="tpu_custom_call" | custom-call | flops 5662310400 | bytes 12000000 | tf_op jit(solution)/shard_map/first_conv_0/pallas_call | solution.py:333
  99.8 0.7 copy-done.19
  100.5 1.3 copy-done.29
  101.8 0.7 copy-done.33
  102.4 0.7 copy-done.35
  103.7 3.1 %copy-done.10 = bf16[640,5760]{1,0:T(8,128)(2,1)S(1)} copy-done((bf16[640,5760]{1,0:T(8,128)(2,1)S(1)}, bf16[640,5760]{1,0:T(8,128)(2,1)}, u32[]{:S(2)}) %copy-start.10) | copy-done | bytes 7372824
  106.8 1.0 copy-done.20
  107.8 1.1 copy-done.23
  108.9 0.9 copy-done.26
  109.8 0.9 copy-done.34
  110.7 0.9 copy-done.36
  111.6 0.8 copy-done.38
  112.5 14.3 %first_conv_1.1 = (f32[640,768]{1,0:T(8,128)S(1)}, f32[128,128]{1,0:T(8,128)}, bf16[640,128]{1,0:T(8,128)(2,1)S(1)}, bf16[640,128]{1,0:T(8,128)(2,1)S(1)}, bf16[640,128]{1,0:T(8,128)(2,1)S(1)}) custom-call(s32[1]{0:T(128)} %bitcast.part_ref, f32[1,128]{1,0:T(1,128)S(1)} %add.68.sums_ref, f32[640,128]{1,0:T(8,128)S(1)} %copy-done.20, ...), custom_call_target="tpu_custom_call" | custom-call | flops 5662310400 | bytes 12000000 | tf_op jit(solution)/shard_map/first_conv_1/pallas_call | solution.py:333
  127.5 1.3 copy-done.27
  128.8 0.7 copy-done.31
  129.5 4.9 %all-to-all-start.2 = ((f32[128,1,128]{2,1,0:T(1,128)}), f32[128,1,128]{2,1,0:T(1,128)S(1)}, u32[]{:S(2)}, u32[]{:S(2)}) async-start(f32[128,1,128]{2,1,0:T(1,128)} %bitcast.13), calls=%async_computation.2 | async-start | bytes 131072 | tf_op jit(solution)/shard_map/all_to_all | solution.py:472
  134.4 4.1 %collective-permute-start.9 = (bf16[640,128]{1,0:T(8,128)(2,1)}, bf16[640,128]{1,0:T(8,128)(2,1)}, u32[]{:S(2)}, u32[]{:S(2)}) collective-permute-start(bf16[640,128]{1,0:T(8,128)(2,1)} %copy-done.22), channel_id=1, source_target_pairs={{0,1},{1,2},{2,3},{3,4},{4,5},{5,6},{6,7},{8,9},{9,10},{10,11},{11... | collective-permute-start | bytes 491528 | tf_op jit(solution)/shard_map/ppermute | solution.py:547
  138.5 1.5 collective-permute-start.10
  140.0 5.2 %copy-done.6 = bf16[2,3,3,640,640]{4,3,2,1,0:T(8,128)(2,1)S(1)} copy-done((bf16[2,3,3,640,640]{4,3,2,1,0:T(8,128)(2,1)S(1)}, bf16[2,3,3,640,640]{4,3,2,1,0:T(8,128)(2,1)}, u32[]{:S(2)}) %copy-start.6) | copy-done | bytes 14745624
  145.2 2.5 %turn_weights_1.1.wv = bf16[640,5760]{1,0:T(8,128)(2,1)S(1)} custom-call(bf16[2,9,640,640]{3,2,1,0:T(8,128)(2,1)S(1)} %bitcast.38), custom_call_target="tpu_custom_call" | custom-call | flops 1887436800 | bytes 15000000 | tf_op jit(solution)/shard_map/turn_weights_1/pallas_call | solution.py:177
  147.7 2.9 %copy-done.11 = bf16[640,5760]{1,0:T(8,128)(2,1)} copy-done((bf16[640,5760]{1,0:T(8,128)(2,1)}, bf16[640,5760]{1,0:T(8,128)(2,1)S(1)}, u32[]{:S(2)}) %copy-start.11) | copy-done | bytes 7372824
  150.6 1.3 turn_target.1.target_hbm
  152.0 1.2 copy-done.17
  153.3 3.1 %copy-done.12 = bf16[640,5760]{1,0:T(8,128)(2,1)S(1)} copy-done((bf16[640,5760]{1,0:T(8,128)(2,1)S(1)}, bf16[640,5760]{1,0:T(8,128)(2,1)}, u32[]{:S(2)}) %copy-start.12) | copy-done | bytes 7372824
  156.3 1.5 copy-done.18
  157.9 1.0 copy-done.21
  158.9 1.0 copy-done.24
  159.9 1.5 copy-done.28
  161.4 1.5 copy-done.30
  163.0 0.9 copy-done.32
  163.9 26.1 %second_conv.1 = (bf16[12,2,64,640]{3,2,1,0:T(8,128)(2,1)}, f32[128,128]{1,0:T(8,128)S(1)}) custom-call(s32[1]{0:T(128)} %bitcast.part_ref, f32[4]{0:T(128)S(1)} %reshape.67.coef_ref, f32[128,128]{1,0:T(8,128)S(1)} %bitcast.39, f32[640,128]{1,0:T(8,128)S(1)} %copy-done.21, bf16[2,128,1024]{2,1,0:T(8,128)(2,1)S(1)} %copy-done.24, ...), custom_call_target="tpu_custom_call" | custom-call | flops 11324620800 | bytes 20000000 | tf_op jit(solution)/shard_map/second_conv/pallas_call | solution.py:428
  190.0 19.9 %all_to_all.20 = f32[128,1,128]{2,1,0:T(1,128)S(1)} all-to-all(f32[128,1,128]{2,1,0:T(1,128)S(1)} %bitcast.40), channel_id=1, replica_groups=mesh['lon'=16,'ch'=8] {'lon','ch'}, dimensions={0} | all-to-all | bytes 131072 | tf_op jit(solution)/shard_map/all_to_all | solution.py:472
  (92 shorter events, 5.8 us)
Async XLA Ops:
  0.6 48.1 %copy-start = (f32[1280,640]{1,0:T(8,128)S(1)}, f32[1280,640]{1,0:T(8,128)}, u32[]{:S(2)}) copy-start(f32[1280,640]{1,0:T(8,128)} %param.22) | copy-start | bytes 9830404
  2.4 9.6 %collective-permute-start.1 = (bf16[2,2,80,96]{3,2,1,0:T(8,128)(2,1)}, bf16[2,2,80,96]{3,2,1,0:T(8,128)(2,1)S(1)}, u32[]{:S(2)}, u32[]{:S(2)}) collective-permute-start(bf16[2,2,80,96]{3,2,1,0:T(8,128)(2,1)} %get-tuple-element.44), channel_id=1, source_target_pairs={{0,120},{8,0},{16,8},{24,16},{32,24},{40,32},{48,40},{56,48},{64,5... | collective-permute-start | bytes 184328 | tf_op jit(solution)/shard_map/ppermute | solution.py:517
  3.8 8.2 %collective-permute-start = (bf16[2,2,80,96]{3,2,1,0:T(8,128)(2,1)S(1)}, bf16[2,2,80,96]{3,2,1,0:T(8,128)(2,1)S(1)}, u32[]{:S(2)}, u32[]{:S(2)}) collective-permute-start(bf16[2,2,80,96]{3,2,1,0:T(8,128)(2,1)S(1)} %get-tuple-element.45), channel_id=1, source_target_pairs={{0,8},{8,16},{16,24},{24,32},{32,40},{40,48},{48,56},{56,64},{64,7... | collective-permute-start | bytes 184328 | tf_op jit(solution)/shard_map/ppermute | solution.py:516
  5.8 24.1 %copy-start.44 = (f32[2]{0:T(128)}, f32[2]{0:T(128)S(1)}, u32[]{:S(2)}) copy-start(f32[2]{0:T(128)S(1)} %get-tuple-element.43) | copy-start | bytes 28
  6.4 1.7 copy-start.1
  8.2 3.8 %copy-start.2 = (bf16[96,2,64,80]{0,3,2,1:T(8,128)(2,1)S(1)}, bf16[96,2,64,80]{0,3,2,1:T(8,128)(2,1)}, u32[]{:S(2)}) copy-start(bf16[96,2,64,80]{0,3,2,1:T(8,128)(2,1)} %param.13) | copy-start | bytes 5898244
  12.3 1.1 copy-start.16
  13.4 6.3 %copy-start.41 = (f32[2,640]{1,0:T(2,128)S(1)}, f32[2,640]{1,0:T(2,128)}, u32[]{:S(2)}) copy-start(f32[2,640]{1,0:T(2,128)} %param.19) | copy-start | bytes 15364
  13.4 30.7 %all-to-all-start = ((bf16[8,8,80,128]{3,2,1,0:T(8,128)(2,1)}), bf16[8,8,80,128]{3,2,1,0:T(8,128)(2,1)}, u32[]{:S(2)}, u32[]{:S(2)}) async-start(bf16[8,8,80,128]{3,2,1,0:T(8,128)(2,1)} %copy-done.16), calls=%async_computation | async-start | bytes 2621440 | tf_op jit(solution)/shard_map/all_to_all | solution.py:482
  19.6 10.3 %copy-start.42 = (s32[2]{0:T(128)S(1)}, s32[2]{0:T(128)}, u32[]{:S(2)}) copy-start(s32[2]{0:T(128)} %param.15) | copy-start | bytes 28
  19.7 1.7 copy-start.3
  25.2 1.1 copy-start.13
  26.3 4.4 %collective-permute-start.2 = (f32[1,128]{1,0:T(1,128)S(1)}, f32[1,128]{1,0:T(1,128)S(1)}, u32[]{:S(2)}, u32[]{:S(2)}) collective-permute-start(f32[1,128]{1,0:T(1,128)S(1)} %get-tuple-element.25), channel_id=1, source_target_pairs={{0,8},{8,0},{16,24},{24,16},{32,40},{40,32},{48,56},{56,48},{64,72... | collective-permute-start | bytes 1544 | tf_op jit(solution)/shard_map/ppermute | solution.py:494
  30.7 2.8 %collective-permute-start.3 = (f32[1,128]{1,0:T(1,128)S(1)}, f32[1,128]{1,0:T(1,128)S(1)}, u32[]{:S(2)}, u32[]{:S(2)}) collective-permute-start(f32[1,128]{1,0:T(1,128)S(1)} %add.62), channel_id=1, source_target_pairs={{0,16},{8,24},{16,0},{24,8},{32,48},{40,56},{48,32},{56,40},{64,80... | collective-permute-start | bytes 1544 | tf_op jit(solution)/shard_map/ppermute | solution.py:494
  30.9 7.4 %copy-start.14 = (bf16[8,8,80,128]{3,2,1,0:T(8,128)(2,1)S(1)}, bf16[8,8,80,128]{3,2,1,0:T(8,128)(2,1)}, u32[]{:S(2)}) copy-start(bf16[8,8,80,128]{3,2,1,0:T(8,128)(2,1)} %copy-done.13) | copy-start | bytes 3932164
  33.5 8.0 %collective-permute-start.4 = (f32[1,128]{1,0:T(1,128)S(1)}, f32[1,128]{1,0:T(1,128)S(1)}, u32[]{:S(2)}, u32[]{:S(2)}) collective-permute-start(f32[1,128]{1,0:T(1,128)S(1)} %add.63), channel_id=1, source_target_pairs={{0,32},{8,40},{16,48},{24,56},{32,0},{40,8},{48,16},{56,24},{64,96... | collective-permute-start | bytes 1544 | tf_op jit(solution)/shard_map/ppermute | solution.py:494
  38.3 1.7 copy-start.4
  40.4 1.1 copy-start.15
  41.5 8.9 %collective-permute-start.5 = (f32[1,128]{1,0:T(1,128)S(1)}, f32[1,128]{1,0:T(1,128)S(1)}, u32[]{:S(2)}, u32[]{:S(2)}) collective-permute-start(f32[1,128]{1,0:T(1,128)S(1)} %add.64), channel_id=1, source_target_pairs={{0,64},{8,72},{16,80},{24,88},{32,96},{40,104},{48,112},{56,120},{... | collective-permute-start | bytes 1544 | tf_op jit(solution)/shard_map/ppermute | solution.py:494
  44.1 59.6 %all-to-all-start.1 = ((bf16[8,8,80,128]{3,2,1,0:T(8,128)(2,1)}), bf16[8,8,80,128]{3,2,1,0:T(8,128)(2,1)}, u32[]{:S(2)}, u32[]{:S(2)}) async-start(bf16[8,8,80,128]{3,2,1,0:T(8,128)(2,1)} %copy-done.15), calls=%async_computation.1 | async-start | bytes 2621440 | tf_op jit(solution)/shard_map/all_to_all | solution.py:482
  48.7 3.2 %copy-start.39 = (f32[2,640]{1,0:T(2,128)S(1)}, f32[2,640]{1,0:T(2,128)}, u32[]{:S(2)}) copy-start(f32[2,640]{1,0:T(2,128)} %param.18) | copy-start | bytes 15364
  48.7 3.2 %copy-start.40 = (f32[2,640]{1,0:T(2,128)S(1)}, f32[2,640]{1,0:T(2,128)}, u32[]{:S(2)}) copy-start(f32[2,640]{1,0:T(2,128)} %param.20) | copy-start | bytes 15364
  50.4 14.3 %collective-permute-start.6 = (f32[1,128]{1,0:T(1,128)S(1)}, f32[1,128]{1,0:T(1,128)S(1)}, u32[]{:S(2)}, u32[]{:S(2)}) collective-permute-start(f32[1,128]{1,0:T(1,128)S(1)} %add.65), channel_id=1, source_target_pairs={{0,1},{1,0},{2,3},{3,2},{4,5},{5,4},{6,7},{7,6},{8,9},{9,8},{10,11... | collective-permute-start | bytes 1544 | tf_op jit(solution)/shard_map/ppermute | solution.py:494
  64.7 13.0 %collective-permute-start.7 = (f32[1,128]{1,0:T(1,128)S(1)}, f32[1,128]{1,0:T(1,128)S(1)}, u32[]{:S(2)}, u32[]{:S(2)}) collective-permute-start(f32[1,128]{1,0:T(1,128)S(1)} %add.66), channel_id=1, source_target_pairs={{0,2},{1,3},{2,0},{3,1},{4,6},{5,7},{6,4},{7,5},{8,10},{9,11},{10,... | collective-permute-start | bytes 1544 | tf_op jit(solution)/shard_map/ppermute | solution.py:494
  67.1 5.2 %copy-start.5 = (bf16[2,3,3,640,640]{4,3,2,1,0:T(8,128)(2,1)S(1)}, bf16[2,3,3,640,640]{4,3,2,1,0:T(8,128)(2,1)}, u32[]{:S(2)}) copy-start(bf16[2,3,3,640,640]{4,3,2,1,0:T(8,128)(2,1)} %param.17) | copy-start | bytes 44236804
  72.2 12.4 %copy-start.25 = (bf16[128,1024]{1,0:T(8,128)(2,1)S(1)}, bf16[128,1024]{1,0:T(8,128)(2,1)}, u32[]{:S(2)}) copy-start(bf16[128,1024]{1,0:T(8,128)(2,1)} %constant.46.clone.pick_ref) | copy-start | bytes 786436
  74.8 2.9 %copy-start.8 = (bf16[640,5760]{1,0:T(8,128)(2,1)}, bf16[640,5760]{1,0:T(8,128)(2,1)S(1)}, u32[]{:S(2)}) copy-start(bf16[640,5760]{1,0:T(8,128)(2,1)S(1)} %turn_weights_0.1.wv) | copy-start | bytes 22118404
  78.3 5.7 %collective-permute-start.8 = (f32[1,128]{1,0:T(1,128)}, f32[1,128]{1,0:T(1,128)}, u32[]{:S(2)}, u32[]{:S(2)}) collective-permute-start(f32[1,128]{1,0:T(1,128)} %add.67), channel_id=1, source_target_pairs={{0,4},{1,5},{2,6},{3,7},{4,0},{5,1},{6,2},{7,3},{8,12},{9,13},{10,... | collective-permute-start | bytes 1544 | tf_op jit(solution)/shard_map/ppermute | solution.py:494
  84.7 3.1 %copy-start.9 = (bf16[640,5760]{1,0:T(8,128)(2,1)S(1)}, bf16[640,5760]{1,0:T(8,128)(2,1)}, u32[]{:S(2)}) copy-start(bf16[640,5760]{1,0:T(8,128)(2,1)} %copy-done.8) | copy-start | bytes 22118404
  99.8 0.7 copy-start.19
  100.5 1.3 copy-start.29
  101.8 0.7 copy-start.33
  102.4 0.7 copy-start.35
  103.1 0.6 copy-start.37
  103.7 3.1 %copy-start.10 = (bf16[640,5760]{1,0:T(8,128)(2,1)S(1)}, bf16[640,5760]{1,0:T(8,128)(2,1)}, u32[]{:S(2)}) copy-start(bf16[640,5760]{1,0:T(8,128)(2,1)} %copy-done.8) | copy-start | bytes 22118404
  106.8 1.0 copy-start.20
  107.8 1.1 copy-start.23
  108.9 0.9 copy-start.26
  109.8 0.9 copy-start.34
  110.7 0.9 copy-start.36
  111.6 0.8 copy-start.38
  126.8 0.7 copy-start.22
  127.5 1.3 copy-start.27
  128.8 0.7 copy-start.31
  129.5 23.8 %all-to-all-start.2 = ((f32[128,1,128]{2,1,0:T(1,128)}), f32[128,1,128]{2,1,0:T(1,128)S(1)}, u32[]{:S(2)}, u32[]{:S(2)}) async-start(f32[128,1,128]{2,1,0:T(1,128)} %bitcast.13), calls=%async_computation.2 | async-start | bytes 131072 | tf_op jit(solution)/shard_map/all_to_all | solution.py:472
  134.4 18.9 %collective-permute-start.9 = (bf16[640,128]{1,0:T(8,128)(2,1)}, bf16[640,128]{1,0:T(8,128)(2,1)}, u32[]{:S(2)}, u32[]{:S(2)}) collective-permute-start(bf16[640,128]{1,0:T(8,128)(2,1)} %copy-done.22), channel_id=1, source_target_pairs={{0,1},{1,2},{2,3},{3,4},{4,5},{5,6},{6,7},{8,9},{9,10},{10,11},{11... | collective-permute-start | bytes 491528 | tf_op jit(solution)/shard_map/ppermute | solution.py:547
  138.5 14.8 %collective-permute-start.10 = (bf16[640,128]{1,0:T(8,128)(2,1)S(1)}, bf16[640,128]{1,0:T(8,128)(2,1)}, u32[]{:S(2)}, u32[]{:S(2)}) collective-permute-start(bf16[640,128]{1,0:T(8,128)(2,1)S(1)} %get-tuple-element.36), channel_id=1, source_target_pairs={{1,0},{2,1},{3,2},{4,3},{5,4},{6,5},{7,6},{9,8},{10,9},{11,10},{12... | collective-permute-start | bytes 491528 | tf_op jit(solution)/shard_map/ppermute | solution.py:548
  140.0 5.2 %copy-start.6 = (bf16[2,3,3,640,640]{4,3,2,1,0:T(8,128)(2,1)S(1)}, bf16[2,3,3,640,640]{4,3,2,1,0:T(8,128)(2,1)}, u32[]{:S(2)}) copy-start(bf16[2,3,3,640,640]{4,3,2,1,0:T(8,128)(2,1)} %param.17) | copy-start | bytes 44236804
  145.2 5.5 %copy-start.7 = (bf16[12,2,64,640]{3,2,1,0:T(8,128)(2,1)S(1)}, bf16[12,2,64,640]{3,2,1,0:T(8,128)(2,1)}, u32[]{:S(2)}) copy-start(bf16[12,2,64,640]{3,2,1,0:T(8,128)(2,1)} %lower_ref) | copy-start | bytes 5898244
  147.7 2.9 %copy-start.11 = (bf16[640,5760]{1,0:T(8,128)(2,1)}, bf16[640,5760]{1,0:T(8,128)(2,1)S(1)}, u32[]{:S(2)}) copy-start(bf16[640,5760]{1,0:T(8,128)(2,1)S(1)} %turn_weights_1.1.wv) | copy-start | bytes 22118404
  152.0 1.3 copy-start.17
  153.2 3.1 %copy-start.12 = (bf16[640,5760]{1,0:T(8,128)(2,1)S(1)}, bf16[640,5760]{1,0:T(8,128)(2,1)}, u32[]{:S(2)}) copy-start(bf16[640,5760]{1,0:T(8,128)(2,1)} %copy-done.11) | copy-start | bytes 22118404
  156.3 1.5 copy-start.18
  157.9 1.0 copy-start.21
  158.9 1.0 copy-start.24
  159.9 1.5 copy-start.28
  161.4 1.5 copy-start.30
  163.0 0.9 copy-start.32
  163.9 46.1 %copy-start.43 = (s32[2]{0:T(128)S(1)}, s32[2]{0:T(128)}, u32[]{:S(2)}) copy-start(s32[2]{0:T(128)} %param.15) | copy-start | bytes 28
  163.9 46.1 %copy-start.45 = (f32[2]{0:T(128)S(1)}, f32[2]{0:T(128)}, u32[]{:S(2)}) copy-start(f32[2]{0:T(128)} %copy-done.44) | copy-start | bytes 28
where the time goes:
time: 212 us; the launch traced here: 211 us
  Pallas kernels  66.9 us (32%)
  local copies, waits for them, and re-layouts  60.9 us (29%)
  starting transfers between devices  38.2 us (18%)
  blocking collectives  19.9 us (9%)
  waiting for transfers between devices  15.5 us (7%)
  other arithmetic  4.23 us (2%)
  matrix products  3.93 us (2%)
    unnamed x92, local copies, waits for them, and re-layouts  55.1 us
    pallas_call x2, Pallas kernels, first_conv(): pl.pallas_call(functools.partial(first_kernel, s), in_specs=[SMEM, VMEM,...  26.3 us
    pallas_call x1, Pallas kernels, second_conv(): pl.pallas_call(second_kernel, in_specs=[SMEM, SMEM] + [VMEM] * 9 + [ANY]...  26.1 us
    all_to_all x1, blocking collectives, everywhere(): lax.all_to_all(rows.reshape(128, 1, 128), ('lon', 'ch'), 0, 0, tiled=True)  19.9 us
    ppermute x7, waiting for transfers between devices, butterfly(): x = x + lax.ppermute(x, axis, pairs)  15.5 us
    ppermute x7, starting transfers between devices, butterfly(): x = x + lax.ppermute(x, axis, pairs)  14.4 us
    all_to_all x2, starting transfers between devices, swap(): return lax.all_to_all(array, axis, split_axis=0, concat_axis=0, tiled=True)  10.7 us
    pallas_call x2, Pallas kernels, pack(): pl.pallas_call(functools.partial(pack_kernel, s), grid=(PART // CHUNK,),...  7.48 us
  transfers between devices with their start and end apart: 14, of which 3 were waited for; matrix products, arithmetic and copies ran while one was open for 5% of the time, Pallas kernels for 12%

commit v1 on v0

v1 whole, which is shorter than its diff:
```python
import functools
import math

import jax
import jax.numpy as jnp
import numpy as np
from jax import lax
from jax.experimental import pallas as pl
from jax.experimental.pallas import tpu as pltpu
from jax.sharding import PartitionSpec as P

GROUPS = 32
C = 640
LAT = 96
ROWS = 12
COLS = 64
SRC = 8
PART = C // SRC
WIDTH = C // GROUPS
TAPS = 9
F32 = jnp.float32
BF16 = jnp.bfloat16
VMEM = pl.BlockSpec(memory_space=pltpu.VMEM)
SMEM = pl.BlockSpec(memory_space=pltpu.SMEM)
ANY = pl.BlockSpec(memory_space=pl.ANY)
CHUNK = 16
LIMIT = 56 * 2**20
SUMS = 96


def roll(x, by):
    by %= 128
    return x if by == 0 else pltpu.roll(x, by, 1)


def side_lanes(of_left, of_right):
    out = np.zeros((128, 1024), np.float32)
    for q in range(-1, 7):
        at = 128 * (q + 1)
        out[of_left(q), at] = 1
        out[of_left(q + 6), at + 64] = 1
        out[of_right(q), at + 63] = 1
        out[of_right(q + 6), at + 127] = 1
    return out.astype(BF16)


def halo_lane(s, side, row):
    return 32 * s + 16 * side + row + 1


def halo_taps():
    out = np.zeros((256, TAPS * 128), np.float32)
    for i in range(3):
        for k in range(3):
            for s in range(2):
                for side in range(2):
                    for row in range(-1, 13):
                        source = 128 * s + 16 * (3 * side + k) + row + i - 1 + 2
                        out[source, 128 * (3 * i + k) + halo_lane(s, side, row)] = 1
    return out.astype(BF16)


def lanes(rows):
    return lax.broadcasted_iota(jnp.int32, (rows, 128), 1)


def members(rows, first, base):
    chan = lax.broadcasted_iota(jnp.int32, (rows, 128), 0) + first
    low = (lanes(rows) - base) * WIDTH
    return (chan >= low) & (chan < low + WIDTH)


def silu(x):
    return 0.5 * x * (1.0 + jnp.tanh(0.5 * x))


def sums_kernel(x_ref, sums_ref, first_ref, last_ref):
    s, c = pl.program_id(0), pl.program_id(1)
    x = x_ref[0].astype(F32)

    @pl.when((s == 0) & (c == 0))
    def _():
        sums_ref[...] = jnp.zeros_like(sums_ref)

    @pl.when(c == 0)
    def _():
        first_ref[0] = x_ref[0, 0:2]

    @pl.when(c == COLS // 16 - 1)
    def _():
        last_ref[0] = x_ref[0, 14:16]

    row = jnp.zeros((1, 128), F32)
    for k in range(2):
        column = jnp.sum(jnp.sum(x * x if k else x, axis=0), axis=1, keepdims=True)
        own = members(PART, 0, 64 * k + 32 * s)
        row += jnp.sum(jnp.where(own, column, 0.0), axis=0, keepdims=True)
    sums_ref[...] += jnp.broadcast_to(row, sums_ref.shape)


def local_sums(latents):
    pair = pl.BlockSpec((1, 2, PART, LAT), lambda s, c: (s, 0, 0, 0))
    return pl.pallas_call(
        sums_kernel,
        grid=(2, COLS // 16),
        in_specs=[pl.BlockSpec((1, 16, PART, LAT), lambda s, c: (s, c, 0, 0))],
        out_specs=[pl.BlockSpec((16, 128), lambda s, c: (0, 0)), pair, pair],
        out_shape=[
            jax.ShapeDtypeStruct((16, 128), F32),
            jax.ShapeDtypeStruct((2, 2, PART, LAT), BF16),
            jax.ShapeDtypeStruct((2, 2, PART, LAT), BF16),
        ],
        compiler_params=pltpu.CompilerParams(vmem_limit_bytes=LIMIT),
        name="local_sums",
    )(latents)


def pack_kernel(main_ref, pay_ref, taken, turned):
    @pl.when((pl.program_id(0) == 0) & (pl.program_id(1) == 0))
    def _():
        taken[...] = jnp.zeros_like(taken)
        turned[...] = jnp.zeros_like(turned)

    taken[:, 0:LAT] = main_ref[0].astype(F32).reshape(COLS * CHUNK, LAT)
    for j in range(CHUNK):
        plain = taken[pl.ds(j, COLS, stride=CHUNK), :]
        both = jnp.concatenate([plain, roll(plain, -6)], axis=0).T
        turned[pl.ds(CHUNK + j, LAT, stride=CHUNK), :] = both[0:LAT, :]

    low = lanes(CHUNK) < 64

    def tile(r):
        return turned[CHUNK * (r + 1) : CHUNK * (r + 2), :]

    for d in range(SRC):
        for q in range(6):
            pay_ref[d, q] = tile(d * ROWS + q).astype(BF16)
        edge = jnp.where(low, tile(d * ROWS - 1), tile(d * ROWS + 6))
        pay_ref[d, 6] = edge.astype(BF16)
        pay_ref[d, 7] = jnp.zeros((CHUNK, 128), BF16)


def pack(latents):
    return pl.pallas_call(
        pack_kernel,
        grid=(2, PART // CHUNK),
        in_specs=[pl.BlockSpec((1, COLS, CHUNK, LAT), lambda s, e: (s, 0, e, 0))],
        out_specs=pl.BlockSpec((SRC, 8, CHUNK, 128), lambda s, e: (0, s, e, 0)),
        out_shape=jax.ShapeDtypeStruct((SRC, 16, PART, 128), BF16),
        scratch_shapes=[
            pltpu.VMEM((COLS * CHUNK, 128), F32),
            pltpu.VMEM(((LAT + 8) * CHUNK, 128), F32),
        ],
        compiler_params=pltpu.CompilerParams(vmem_limit_bytes=LIMIT),
        cost_estimate=pl.CostEstimate(
            flops=1_000_000_000, bytes_accessed=8_000_000, transcendentals=0
        ),
        name="pack_latents",
    )(latents)


def halo_kernel(sums_ref, left_ref, first_ref, last_ref, right_ref, _, pay_ref):
    s = pl.program_id(0)
    lane = lanes(PART)
    pad = jnp.zeros((PART, 128 - LAT), F32)
    near = [left_ref[0, 0], left_ref[0, 1], first_ref[0, 0], last_ref[0, 0],
            right_ref[0, 0], right_ref[0, 1]]
    near = [jnp.concatenate([col.astype(F32), pad], axis=1) for col in near]
    row = jnp.sum(sums_ref[...], axis=0, keepdims=True)
    carried = jnp.zeros((PART, 128), F32)
    for k in range(2):
        own = members(PART, 0, 64 * k + 32 * s)
        value = jnp.sum(jnp.where(own, row, 0.0), axis=1, keepdims=True)
        for piece in range(3):
            part = value.astype(BF16).astype(F32)
            carried = jnp.where(lane == SUMS + 3 * k + piece, part, carried)
            value = value - part
    for d in range(SRC):
        halo = carried
        for kind in range(6):
            own = (lane >= 16 * kind) & (lane < 16 * kind + 16)
            halo = jnp.where(own, roll(near[kind], 16 * kind + 2 - d * ROWS), halo)
        pay_ref[d, 0] = halo.astype(BF16)


def pack_halo(sums, latents, left, right, pay):
    pair = (1, 2, PART, LAT)
    one = (1, 1, PART, LAT)
    return pl.pallas_call(
        halo_kernel,
        grid=(2,),
        in_specs=[
            pl.BlockSpec((16, 128), lambda s: (0, 0)),
            pl.BlockSpec(pair, lambda s: (s, 0, 0, 0)),
            pl.BlockSpec(one, lambda s: (s, 0, 0, 0)),
            pl.BlockSpec(one, lambda s: (s, COLS - 1, 0, 0)),
            pl.BlockSpec(pair, lambda s: (s, 0, 0, 0)),
            ANY,
        ],
        out_specs=pl.BlockSpec((SRC, 1, PART, 128), lambda s: (0, 8 * s + 7, 0, 0)),
        out_shape=jax.ShapeDtypeStruct((SRC, 16, PART, 128), BF16),
        input_output_aliases={5: 0},
        compiler_params=pltpu.CompilerParams(vmem_limit_bytes=LIMIT),
        name="pack_halo",
    )(sums, left, latents, latents, right, pay)


def weight_kernel(w_ref, o_ref):
    o_ref[...] = w_ref[0, 0].T


def turn_weights(j, weights):
    taps = weights.reshape(2, TAPS, C, C)
    return pl.pallas_call(
        weight_kernel,
        grid=(TAPS,),
        in_specs=[pl.BlockSpec((1, 1, C, C), lambda t: (j, t, 0, 0))],
        out_specs=pl.BlockSpec((C, C), lambda t: (0, t)),
        out_shape=jax.ShapeDtypeStruct((C, TAPS * C), BF16),
        compiler_params=pltpu.CompilerParams(vmem_limit_bytes=LIMIT),
        cost_estimate=pl.CostEstimate(
            flops=TAPS * 2 * C * C * 256, bytes_accessed=15_000_000, transcendentals=0
        ),
        name=f"turn_weights_{j}",
    )(taps)


def target_kernel(upper_ref, lower_ref, o_ref):
    o_ref[0, 0] = jnp.concatenate([upper_ref[0, 0], lower_ref[0, 0]], axis=0).T


def turn_target(target):
    block = (1, 1, COLS, C)
    return pl.pallas_call(
        target_kernel,
        grid=(2, 6),
        in_specs=[
            pl.BlockSpec(block, lambda s, q: (q, s, 0, 0)),
            pl.BlockSpec(block, lambda s, q: (q + 6, s, 0, 0)),
        ],
        out_specs=pl.BlockSpec((1, 1, C, 128), lambda s, q: (s, q, 0, 0)),
        out_shape=jax.ShapeDtypeStruct((2, 6, C, 128), BF16),
        compiler_params=pltpu.CompilerParams(vmem_limit_bytes=LIMIT),
        name="turn_target",
    )(target, target)


def affine(total, square, par_ref, j, scale, offset):
    count = float(LAT * 1024 * WIDTH)
    mean = total / count
    spread = square / count - mean * mean
    factor = lax.rsqrt(spread + 1e-05) * par_ref[:, 2 * j : 2 * j + 1]
    rest = par_ref[:, 2 * j + 1 : 2 * j + 2] - mean * factor
    scale[...] = jnp.broadcast_to(factor, scale.shape)
    offset[...] = jnp.broadcast_to(rest, offset.shape)


def spread_taps(xs, at, tiles, edge, sides, part):
    rows = PART
    lane = lanes(rows)
    low = lane < 64
    first = (lane == 0) | (lane == 64)
    last = (lane == 63) | (lane == 127)
    for q in range(-1, 7):
        if q == -1:
            tile = jnp.where(low, edge, roll(tiles[5], 64))
        elif q == 6:
            tile = jnp.where(low, roll(tiles[0], 64), edge)
        else:
            tile = tiles[q]
        side = sides[pl.ds(at, rows), 128 * (q + 1) : 128 * (q + 2)]
        taps = (jnp.where(first, side, roll(tile, 1)), tile, jnp.where(last, side, roll(tile, -1)))
        for k, tap in enumerate(taps):
            if q == -1:
                tap = jnp.where(low & (part == 0), 0.0, tap)
            elif q == 6:
                tap = jnp.where((~low) & (part == SRC - 1), 0.0, tap)
            xs[pl.ds(k * C + at, rows), 128 * (q + 1) : 128 * (q + 2)] = tap.astype(BF16)


def product(wv, xs, n):
    x = jnp.concatenate([xs[:, n + 128 * i : n + 128 * i + 256] for i in range(3)], axis=0)
    return jnp.dot(wv[...], x, preferred_element_type=F32)


def first_kernel(
    part_ref, par_ref, pick_ref, taps_ref, recv_hbm, w_hbm,
    hid_hbm, out_sums, to_next, to_prev, out_halo,
    xs, wv, scale, offset, recv, hid, sides, xh, sems,
):
    fetches = [
        pltpu.make_async_copy(recv_hbm.at[:, 8 * s : 8 * s + 8], recv.at[s], sems.at[s])
        for s in range(2)
    ]
    weights = pltpu.make_async_copy(w_hbm, wv, sems.at[2])
    for copy in (*fetches, weights):
        copy.start()
    part = part_ref[0]
    lane = lanes(C)

    def act(x, a, o):
        return silu(x.astype(F32) * a + o)

    def columns(s):
        fetches[s].wait()
        tile = recv[s, :, 7].reshape(C, 128).astype(F32)
        total, square = (
            jnp.sum(jnp.where((lane >= at) & (lane < at + 3), tile, 0.0), axis=1, keepdims=True)
            for at in (SUMS, SUMS + 3)
        )
        affine(total, square, par_ref, 0, scale.at[s], offset.at[s])
        r = (lane & 15) - 2
        unused = lane >= SUMS
        outside = ((part == 0) & (r < 0)) | ((part == SRC - 1) & (r >= ROWS)) | unused
        x = jnp.where(unused, 0.0, tile)
        halo = jnp.where(outside, 0.0, act(x, scale[s], offset[s])).astype(BF16)
        sides[s] = jnp.dot(halo, pick_ref[...], preferred_element_type=F32)
        return halo

    def prepare(s, b):
        at = b * PART if isinstance(b, int) else pl.multiple_of(b * PART, PART)
        a, o = scale[s, pl.ds(at, PART), :], offset[s, pl.ds(at, PART), :]
        tiles = [act(recv[s, b, q], a, o) for q in range(7)]
        spread_taps(xs.at[s], at, tiles[:6], tiles[6], sides.at[s], part)

    halo = columns(0)

    @pl.loop(0, SRC)
    def _(b):
        prepare(0, b)

    both = jnp.concatenate([halo, columns(1)], axis=1)
    for t in range(TAPS):
        picked = jnp.dot(both, taps_ref[:, 128 * t : 128 * t + 128], preferred_element_type=F32)
        xh[C * t : C * (t + 1), :] = picked.astype(BF16)

    weights.wait()
    stores = []

    def put(s):
        store = pltpu.make_async_copy(hid.at[s], hid_hbm.at[s], sems.at[s])
        store.start()
        stores.append(store)

    for c, blocks in enumerate(((0, 1, 2), (3, 4, 5), (6, 7))):
        n = 256 * c
        hid[0, :, n : n + 256] = product(wv, xs.at[0], n) + par_ref[:, 5:6]
        for b in blocks:
            prepare(1, b)
    put(0)
    for n in range(0, 768, 256):
        hid[1, :, n : n + 256] = product(wv, xs.at[1], n) + par_ref[:, 6:7]
    put(1)
    halo = jnp.dot(wv[...], xh[...], preferred_element_type=F32)
    bias = jnp.where(lane < 32, par_ref[:, 5:6], par_ref[:, 6:7])
    out_halo[...] = (halo + bias).astype(BF16)

    row = jnp.zeros((1, 128), F32)
    low = lanes(128) < 64
    for at in range(0, C, 128):
        for s in range(2):
            pieces = [hid[s, at : at + 128, 128 * q : 128 * (q + 1)] for q in range(6)]
            for k in range(2):
                column = jnp.sum(sum(p * p if k else p for p in pieces), axis=1, keepdims=True)
                own = members(128, at, 64 * k + 32 * s)
                row += jnp.sum(jnp.where(own, column, 0.0), axis=0, keepdims=True)
        start, end = hid.at[:, at : at + 128, 0:128], hid.at[:, at : at + 128, 640:768]
        to_next[at : at + 128, :] = jnp.where(low, roll(end[0], 64), end[1]).astype(BF16)
        to_prev[at : at + 128, :] = jnp.where(low, start[0], roll(start[1], 64)).astype(BF16)
    out_sums[...] = jnp.broadcast_to(row, out_sums.shape)
    for store in stores:
        store.wait()


def first_conv(part, params, pick, taps, recv, weights):
    tile = jax.ShapeDtypeStruct((C, 128), BF16)
    return pl.pallas_call(
        first_kernel,
        in_specs=[SMEM, VMEM, VMEM, VMEM, ANY, ANY],
        out_specs=[ANY] + [VMEM] * 4,
        out_shape=[
            jax.ShapeDtypeStruct((2, C, 768), F32),
            jax.ShapeDtypeStruct((128, 128), F32),
            tile, tile, tile,
        ],
        scratch_shapes=[
            pltpu.VMEM((2, 3 * C, 1024), BF16),
            pltpu.VMEM((C, TAPS * C), BF16),
            pltpu.VMEM((2, C, 128), F32),
            pltpu.VMEM((2, C, 128), F32),
            pltpu.VMEM((2, SRC, 8, PART, 128), BF16),
            pltpu.VMEM((2, C, 768), F32),
            pltpu.VMEM((2, C, 1024), F32),
            pltpu.VMEM((TAPS * C, 128), BF16),
            pltpu.SemaphoreType.DMA((3,)),
        ],
        compiler_params=pltpu.CompilerParams(vmem_limit_bytes=LIMIT),
        cost_estimate=pl.CostEstimate(
            flops=4 * 768 * C * C * 9, bytes_accessed=20_000_000, transcendentals=0
        ),
        name="first_conv",
    )(part, params, pick, taps, recv, weights)


def second_kernel(
    part_ref, coef_ref, sums_ref, par_ref, pick_ref, near_ref, prev_ref, next_ref,
    hid_hbm, w_hbm, recv_hbm, target_hbm,
    noise_hbm, out_ref,
    xs, wv, hid, lat, target, noise_out, sides, scale, offset, sems,
):
    weights = pltpu.make_async_copy(w_hbm, wv, sems.at[8])
    fetches, later = [], []
    for s in range(2):
        fetches.append(pltpu.make_async_copy(hid_hbm.at[s], hid.at[s], sems.at[s]))
        tiles = recv_hbm.at[:, 8 * s : 8 * s + 6]
        later.append(pltpu.make_async_copy(tiles, lat.at[s], sems.at[2 + s]))
        later.append(pltpu.make_async_copy(target_hbm.at[s], target.at[s], sems.at[4 + s]))
    for copy in (fetches[0], weights, fetches[1], *later):
        copy.start()
    part = part_ref[0]
    row = jnp.sum(sums_ref[...], axis=0, keepdims=True)
    low = lanes(PART) < 64

    def columns(s):
        total, square = (
            jnp.sum(jnp.where(members(C, 0, base), row, 0.0), axis=1, keepdims=True)
            for base in (32 * s, 64 + 32 * s)
        )
        affine(total, square, par_ref, 1, scale.at[s], offset.at[s])
        halo = silu(near_ref[...].astype(F32) * scale[s] + offset[s]).astype(BF16)
        sides[s] = jnp.dot(halo, pick_ref[s], preferred_element_type=F32)
        fetches[s].wait()

    def prepare(s, b):
        at = b * PART if isinstance(b, int) else pl.multiple_of(b * PART, PART)
        rows = pl.ds(at, PART)
        a, o = scale[s, rows, :], offset[s, rows, :]

        def act(x):
            return silu(x * a + o)

        tiles = [act(hid[s, rows, 128 * q : 128 * (q + 1)]) for q in range(6)]
        above, below = prev_ref[rows, :].astype(F32), next_ref[rows, :].astype(F32)
        if s == 0:
            edge = jnp.where(low, above, roll(below, 64))
        else:
            edge = jnp.where(low, roll(above, 64), below)
        spread_taps(xs.at[s], at, tiles, act(edge), sides.at[s], part)

    def finish(s, n, acc):
        keep, gain = coef_ref[2 * s], coef_ref[2 * s + 1]
        out = product(wv, xs.at[s], n) + par_ref[:, 4:5]
        for h in range(2):
            q = n // 128 + h
            mine = lat[s, :, q].reshape(C, 128).astype(F32)
            noise = (out[:, 128 * h : 128 * h + 128] + mine).astype(BF16)
            center = keep * mine + gain * noise.astype(F32)
            diff = target[s, q].astype(F32) - center
            acc += jnp.sum((diff * diff).reshape(C // 8, 8, 128), axis=0)
            plain = noise.T
            noise_out[s, q] = plain[0:64]
            noise_out[s, q + 6] = plain[64:128]
        return acc

    columns(0)

    @pl.loop(0, SRC)
    def _(b):
        prepare(0, b)

    columns(1)
    weights.wait()
    for copy in later:
        copy.wait()
    result = jnp.zeros((1, 128), F32)
    stores = []
    for s in range(2):
        acc = jnp.zeros((8, 128), F32)
        for c, blocks in enumerate(((0, 1, 2), (3, 4, 5), (6, 7))):
            acc = finish(s, 256 * c, acc)
            if s == 0:
                for b in blocks:
                    prepare(1, b)
        store = pltpu.make_async_copy(noise_out.at[s], noise_hbm.at[:, s], sems.at[6 + s])
        store.start()
        stores.append(store)
        value = jnp.sum(acc, axis=(0, 1), keepdims=True)
        result = jnp.where(lanes(1) == s, value, result)
    out_ref[...] = jnp.broadcast_to(result, out_ref.shape)
    for store in stores:
        store.wait()


def second_conv(part, coef, sums, params, pick, tiles, hidden, weights, recv, target):
    return pl.pallas_call(
        second_kernel,
        in_specs=[SMEM, SMEM] + [VMEM] * 6 + [ANY] * 4,
        out_specs=[ANY, VMEM],
        out_shape=[
            jax.ShapeDtypeStruct((ROWS, 2, COLS, C), BF16),
            jax.ShapeDtypeStruct((128, 128), F32),
        ],
        scratch_shapes=[
            pltpu.VMEM((2, 3 * C, 1024), BF16),
            pltpu.VMEM((C, TAPS * C), BF16),
            pltpu.VMEM((2, C, 768), F32),
            pltpu.VMEM((2, SRC, 6, PART, 128), BF16),
            pltpu.VMEM((2, 6, C, 128), BF16),
            pltpu.VMEM((2, ROWS, COLS, C), BF16),
            pltpu.VMEM((2, C, 1024), F32),
            pltpu.VMEM((2, C, 128), F32),
            pltpu.VMEM((2, C, 128), F32),
            pltpu.SemaphoreType.DMA((9,)),
        ],
        compiler_params=pltpu.CompilerParams(vmem_limit_bytes=LIMIT),
        cost_estimate=pl.CostEstimate(
            flops=4 * 768 * C * C * 9, bytes_accessed=20_000_000, transcendentals=0
        ),
        name="second_conv",
    )(part, coef, sums, params, pick, *tiles, hidden, weights, recv, target)


def time_embed(timesteps, time_w1, time_w2):
    half = time_w1.shape[0] // 2
    freqs = jnp.exp(-math.log(10000.0) * jnp.arange(half, dtype=F32) / half)
    angles = timesteps.astype(F32)[:, None] * freqs[None, :]
    features = jnp.concatenate([jnp.cos(angles), jnp.sin(angles)], axis=1)
    hidden = jax.nn.silu(jnp.dot(features, time_w1, precision=lax.Precision.HIGHEST))
    return jnp.dot(hidden, time_w2, precision=lax.Precision.HIGHEST)


def plan(steps):
    frac = steps.astype(F32) / 1000.0
    return jnp.cos((frac + 0.008) / 1.008 * (math.pi / 2.0)) ** 2


def everywhere(rows, axes):
    got = lax.all_to_all(rows.reshape(-1, 1, 128), axes, 0, 0, tiled=True)
    return got.reshape(-1, 128)


def ring(axis, step, wrap):
    size = lax.axis_size(axis)
    return [(i, (i + step) % size) for i in range(size) if wrap or 0 <= i + step < size]


def swap(array, axis):
    return lax.all_to_all(array, axis, split_axis=0, concat_axis=0, tiled=True)


def after(value, *others):
    return lax.optimization_barrier((value,) + others)[0]


def body(
    latents, next_latents, timesteps, resume_steps, conv_weights, conv_bias,
    norm_gain, norm_shift, time_w1, time_w2,
):
    part = lax.axis_index("ch").astype(jnp.int32).reshape(1)
    first_pick = jnp.asarray(side_lanes(lambda r: 16 + r + 2, lambda r: 64 + r + 2))
    second_pick = jnp.asarray(
        np.stack(
            [
                side_lanes(lambda r: halo_lane(s, 0, r), lambda r: halo_lane(s, 1, r))
                for s in range(2)
            ]
        )
    )
    tap_pick = jnp.asarray(halo_taps())

    cells = latents.transpose(1, 2, 3, 0)
    sums, first, last = local_sums(cells)
    sums = everywhere(sums, "lon")
    left = lax.ppermute(last, "lon", ring("lon", 1, True))
    right = lax.ppermute(first, "lon", ring("lon", -1, True))
    pay = pack(after(cells, first))
    pay = pack_halo(sums, cells, left, right, pay)
    recv = swap(pay, "ch")
    conv_weights, time_w1, following = after((conv_weights, time_w1, next_latents), pay)
    turned = [turn_weights(j, conv_weights) for j in range(2)]
    target = turn_target(following)

    temb = time_embed(timesteps, time_w1, time_w2)
    columns = [
        norm_gain[0], norm_shift[0], norm_gain[1], norm_shift[1], conv_bias[1],
        conv_bias[0] + temb[0], conv_bias[0] + temb[1],
    ]
    params = jnp.pad(jnp.stack(columns, axis=1), ((0, 0), (0, 128 - len(columns))))

    alpha = plan(timesteps)
    prior = plan(timesteps - resume_steps)
    variance = (1.0 - prior) / (1.0 - alpha) * (1.0 - alpha / prior)
    keep = (1.0 - prior) * jnp.sqrt(alpha / (prior * (1.0 - alpha)))
    ratio = jnp.sqrt(prior) / jnp.sqrt(alpha)
    coef = jnp.stack([ratio, keep - ratio * jnp.sqrt(1.0 - alpha)], axis=1).reshape(4)

    hidden, sums, to_next, to_prev, near = first_conv(
        part, params, first_pick, tap_pick, recv, turned[0]
    )
    from_prev = lax.ppermute(to_next, "ch", ring("ch", 1, False))
    from_next = lax.ppermute(to_prev, "ch", ring("ch", -1, False))
    sums = everywhere(sums, ("lon", "ch"))
    noise, terms = second_conv(
        part, coef, sums, params, second_pick, (near, from_prev, from_next),
        hidden, turned[1], recv, target,
    )
    squares = jnp.sum(everywhere(terms, ("lon", "ch")), axis=0)[:2]
    logprob = (
        -squares / (2.0 * variance) / float(LAT * 1024 * C)
        - 0.5 * jnp.log(variance)
        - 0.5 * math.log(2.0 * math.pi)
    )
    return (noise, logprob)


def solution(mesh):
    return jax.shard_map(
        body,
        mesh=mesh,
        in_specs=(
            P(None, None, "lon", "ch"),
            P("ch", None, "lon", None),
            P(), P(), P(), P(), P(), P(), P(), P(),
        ),
        out_specs=(P("ch", None, "lon", None), P()),
        check_vma=False,
    )
```

time: 212 us -> 175 us (0.83)
  local copies, waits for them, and re-layouts: 60.9 us -> 4.75 us
  Pallas kernels: 66.9 us -> 95.5 us
  starting transfers between devices: 38.2 us -> 33.6 us
  other arithmetic: 4.23 us -> 1.01 us
    unnamed x92 -> x22, local copies, waits for them, and re-layouts: 55.1 us -> 1.33 us
    all_to_all x1 -> x2, starting transfers between devices: 4.91 us -> 22.3 us  [everywhere(): got = lax.all_to_all(rows.reshape(-1, 1, 128), axes, 0, 0, tiled=True)]
    pallas_call x2, Pallas kernels: 5.02 us -> 21 us  [turn_weights(): pl.pallas_call(weight_kernel, grid=(TAPS,), in_specs=[pl.BlockSpec((1, 1,...]
    ppermute x9 -> x2, waiting for transfers between devices: 15.5 us -> 0.01 us  [the longest x1 0.01 us: body(): right = lax.ppermute(first, 'lon', ring('lon', -1, True))]
    ppermute x9 -> x2, starting transfers between devices: 17 us -> 2.68 us  [the longest x1 1.42 us: body(): right = lax.ppermute(first, 'lon', ring('lon', -1, True))]
    all_to_all x2 -> x1, waiting for transfers between devices: 0.01 us -> 14.2 us  [swap(): return lax.all_to_all(array, axis, split_axis=0, concat_axis=0, tiled=True)]
    pallas_call x1, Pallas kernels: 1.35 us -> 7.95 us  [turn_target(): pl.pallas_call(target_kernel, grid=(2, 6), in_specs=[pl.BlockSpec(block,...]
    pallas_call x7 -> x5, Pallas kernels: 60.6 us -> 66.6 us  [the longest x1 26.9 us: first_conv(): pl.pallas_call(first_kernel, in_specs=[SMEM, VMEM, VMEM, VMEM, ANY, ANY],...]
  transfers between devices with their start and end apart: 14 -> 7, of which waited for: 3 -> 1; matrix products, arithmetic and copies ran while one was open for 5% -> 4% of each run, Pallas kernels for 12% -> 22%
where the time goes in v1:
time: 175 us; the launch traced here: 173 us
  Pallas kernels  95.5 us (55%)
  starting transfers between devices  33.6 us (19%)
  blocking collectives  19.4 us (11%)
  waiting for transfers between devices  14.2 us (8%)
  local copies, waits for them, and re-layouts  4.75 us (3%)
  matrix products  3.94 us (2%)
    pallas_call x1, Pallas kernels, first_conv(): pl.pallas_call(first_kernel, in_specs=[SMEM, VMEM, VMEM, VMEM, ANY, ANY],...  26.9 us
    all_to_all x2, starting transfers between devices, everywhere(): got = lax.all_to_all(rows.reshape(-1, 1, 128), axes, 0, 0, tiled=True)  22.3 us
    pallas_call x1, Pallas kernels, second_conv(): pl.pallas_call(second_kernel, in_specs=[SMEM, SMEM] + [VMEM] * 6 + [ANY]...  21.7 us
    pallas_call x2, Pallas kernels, turn_weights(): pl.pallas_call(weight_kernel, grid=(TAPS,), in_specs=[pl.BlockSpec((1, 1,...  21 us
    all_to_all x1, blocking collectives, everywhere(): got = lax.all_to_all(rows.reshape(-1, 1, 128), axes, 0, 0, tiled=True)  19.4 us
    all_to_all x1, waiting for transfers between devices, swap(): return lax.all_to_all(array, axis, split_axis=0, concat_axis=0, tiled=True)  14.2 us
    pallas_call x1, Pallas kernels, pack(): pl.pallas_call(pack_kernel, grid=(2, PART // CHUNK), in_specs=[pl.BlockSp...  9.73 us
    pallas_call x1, Pallas kernels, turn_target(): pl.pallas_call(target_kernel, grid=(2, 6), in_specs=[pl.BlockSpec(block,...  7.95 us
  transfers between devices with their start and end apart: 7, of which 1 were waited for; matrix products, arithmetic and copies ran while one was open for 4% of the time, Pallas kernels for 22%

profile of v1, /device:TPU:1, one launch (start us, length us, event | category | flops | bytes accessed | tf_op | source)
XLA Modules:
  0.0 173.2 jit_solution(6040094416414838757)
XLA Ops:
  0.6 0.0 copy-start
  0.6 6.0 %local_sums.1 = (f32[16,128]{1,0:T(8,128)}, bf16[2,2,80,96]{3,2,1,0:T(8,128)(2,1)}, bf16[2,2,80,96]{3,2,1,0:T(8,128)(2,1)}) custom-call(bf16[2,64,80,96]{3,2,1,0:T(8,128)(2,1)} %bitcast.36), custom_call_target="tpu_custom_call" | custom-call | tf_op jit(solution)/shard_map/local_sums/pallas_call | solution.py:103
  6.6 1.4 collective-permute-start.1
  8.1 1.3 collective-permute-start
  9.3 10.3 %all-to-all-start = ((f32[16,1,128]{2,1,0:T(1,128)}), f32[16,1,128]{2,1,0:T(1,128)S(1)}, u32[]{:S(2)}, u32[]{:S(2)}) async-start(f32[16,1,128]{2,1,0:T(1,128)} %bitcast.44), calls=%async_computation | async-start | bytes 16384 | tf_op jit(solution)/shard_map/all_to_all | solution.py:538
  19.6 9.7 %pack_latents.1._ = bf16[8,16,80,128]{3,2,1,0:T(8,128)(2,1)} custom-call(bf16[2,64,80,96]{3,2,1,0:T(8,128)(2,1)} %bitcast.37), custom_call_target="tpu_custom_call" | custom-call | flops 1000000000 | bytes 8000000 | tf_op jit(solution)/shard_map/pack_latents/pallas_call | solution.py:144
  29.4 0.0 all-to-all-done
  29.4 0.0 copy-start.4
  29.4 0.0 collective-permute-done.1.right_ref
  29.4 0.0 copy-start.1
  29.4 0.0 collective-permute-done.left_ref
  29.4 0.0 copy-start.2
  29.4 0.6 copy-done.4
  30.0 0.0 copy-done.1
  30.0 0.0 copy-done.2
  30.0 2.3 %pack_halo.1 = bf16[8,16,80,128]{3,2,1,0:T(8,128)(2,1)} custom-call(f32[16,128]{1,0:T(8,128)} %bitcast.43, bf16[2,2,80,96]{3,2,1,0:T(8,128)(2,1)} %copy-done.2, bf16[2,64,80,96]{3,2,1,0:T(8,128)(2,1)} %bitcast.38, bf16[2,64,80,96]{3,2,1,0:T(8,128)(2,1)} %bitcast.39, bf16[2,2,80,96]{3,2,1,0:T(8,128)(2,1)} %copy-done.1, ...), custom_call_target="tpu_custom_call", output_to_operand_aliasing={{}: (5, {})} | custom-call | tf_op jit(solution)/shard_map/pack_halo/pallas_call | solution.py:189
  32.3 0.0 copy-start.8
  32.3 0.0 copy-start.9
  32.3 0.0 copy-start.7
  32.3 5.3 %all-to-all-start.1 = ((bf16[8,16,80,128]{3,2,1,0:T(8,128)(2,1)}), bf16[8,16,80,128]{3,2,1,0:T(8,128)(2,1)}, u32[]{:S(2)}, u32[]{:S(2)}) async-start(bf16[8,16,80,128]{3,2,1,0:T(8,128)(2,1)} %pack_halo.1), calls=%async_computation.1 | async-start | bytes 5242880 | tf_op jit(solution)/shard_map/all_to_all | solution.py:548
  37.6 0.0 copy-start.5
  37.6 0.0 copy-start.6
  37.7 0.0 copy-done.8
  37.7 0.0 copy-done.9
  37.7 0.1 fusion.11
  37.8 0.1 subtract_bitcast_fusion
  37.8 0.1 copy.25
  37.9 0.7 reshape.73.coef_ref
  38.6 0.1 multiply_cosine_fusion
  38.7 0.0 copy-done.7
  38.8 2.3 %fusion.5 = f32[2,1280]{1,0:T(2,128)S(1)} fusion(f32[320,1280]{1,0:T(8,128)} %param.21, f32[2,160]{1,0:T(2,128)S(1)} %get-tuple-element.40, f32[2,160]{1,0:T(2,128)S(1)} %get-tuple-element.39), kind=kOutput, calls=%fused_computation.6 | convolution fusion | flops 9831040 | bytes 1651200 | tf_op jit(solution)/shard_map/dot_general | solution.py:528
  41.0 0.0 copy-done
  41.0 1.7 fusion
  42.7 0.0 copy-done.5
  42.7 0.0 copy-done.6
  42.8 0.9 copy.27
  43.7 1.7 pad.4.par_ref
  45.4 10.5 %turn_weights_0.1.w_hbm = bf16[640,5760]{1,0:T(8,128)(2,1)} custom-call(bf16[2,9,640,640]{3,2,1,0:T(8,128)(2,1)} %bitcast.34), custom_call_target="tpu_custom_call" | custom-call | flops 1887436800 | bytes 15000000 | tf_op jit(solution)/shard_map/turn_weights_0/pallas_call | solution.py:214
  55.9 14.2 %all-to-all-done.1.recv_hbm = bf16[8,16,80,128]{3,2,1,0:T(8,128)(2,1)} async-done(((bf16[8,16,80,128]{3,2,1,0:T(8,128)(2,1)}), bf16[8,16,80,128]{3,2,1,0:T(8,128)(2,1)}, u32[]{:S(2)}, u32[]{:S(2)}) %all-to-all-start.1) | async-done | bytes 2621472 | tf_op jit(solution)/shard_map/all_to_all | solution.py:548
  70.0 26.9 %first_conv.1 = (f32[2,640,768]{2,1,0:T(8,128)}, f32[128,128]{1,0:T(8,128)}, bf16[640,128]{1,0:T(8,128)(2,1)}, bf16[640,128]{1,0:T(8,128)(2,1)}, bf16[640,128]{1,0:T(8,128)(2,1)}) custom-call(s32[1]{0:T(128)} %bitcast.part_ref, f32[640,128]{1,0:T(8,128)} %pad.4.par_ref, bf16[128,1024]{1,0:T(8,128)(2,1)} %constant.46.clone.pick_ref, ...), custom_call_target="tpu_custom_call" | custom-call | flops 11324620800 | bytes 20000000 | tf_op jit(solution)/shard_map/first_conv/pallas_call | solution.py:377
  96.9 2.0 %collective-permute-start.2 = (bf16[640,128]{1,0:T(8,128)(2,1)}, bf16[640,128]{1,0:T(8,128)(2,1)S(1)}, u32[]{:S(2)}, u32[]{:S(2)}) collective-permute-start(bf16[640,128]{1,0:T(8,128)(2,1)} %get-tuple-element.24), channel_id=1, source_target_pairs={{0,1},{1,2},{2,3},{3,4},{4,5},{5,6},{6,7},{8,9},{9,10},{10,11},{11... | collective-permute-start | bytes 491528 | tf_op jit(solution)/shard_map/ppermute | solution.py:600
  99.0 1.3 collective-permute-start.3
  100.3 12.0 %all-to-all-start.2 = ((f32[128,1,128]{2,1,0:T(1,128)}), f32[128,1,128]{2,1,0:T(1,128)S(1)}, u32[]{:S(2)}, u32[]{:S(2)}) async-start(f32[128,1,128]{2,1,0:T(1,128)} %bitcast.41), calls=%async_computation.2 | async-start | bytes 131072 | tf_op jit(solution)/shard_map/all_to_all | solution.py:538
  112.3 10.5 %turn_weights_1.1.w_hbm = bf16[640,5760]{1,0:T(8,128)(2,1)} custom-call(bf16[2,9,640,640]{3,2,1,0:T(8,128)(2,1)} %bitcast.35), custom_call_target="tpu_custom_call" | custom-call | flops 1887436800 | bytes 15000000 | tf_op jit(solution)/shard_map/turn_weights_1/pallas_call | solution.py:214
  122.8 7.9 %turn_target.1.target_hbm = bf16[2,6,640,128]{3,2,1,0:T(8,128)(2,1)} custom-call(bf16[12,2,64,640]{3,2,1,0:T(8,128)(2,1)} %lower_ref, bf16[12,2,64,640]{3,2,1,0:T(8,128)(2,1)} %lower_ref), custom_call_target="tpu_custom_call" | custom-call | tf_op jit(solution)/shard_map/turn_target/pallas_call | solution.py:234
  130.7 0.0 all-to-all-done.2
  130.7 0.0 copy-start.3
  130.7 0.0 collective-permute-done.2.prev_ref
  130.7 0.0 copy-start.10
  130.7 0.0 collective-permute-done.3.next_ref
  130.7 0.6 copy-done.3
  131.3 0.1 copy-done.10
  131.4 21.7 %second_conv.1 = (bf16[12,2,64,640]{3,2,1,0:T(8,128)(2,1)}, f32[128,128]{1,0:T(8,128)}) custom-call(s32[1]{0:T(128)} %bitcast.part_ref, f32[4]{0:T(128)} %reshape.73.coef_ref, f32[128,128]{1,0:T(8,128)} %bitcast.40, f32[640,128]{1,0:T(8,128)} %pad.4.par_ref, bf16[2,128,1024]{2,1,0:T(8,128)(2,1)} %constant.47.clone.pick_ref, ...), custom_call_target="tpu_custom_call" | custom-call | flops 11324620800 | bytes 20000000 | tf_op jit(solution)/shard_map/second_conv/pallas_call | solution.py:495
  153.1 19.4 %all_to_all.20 = f32[128,1,128]{2,1,0:T(1,128)S(1)} all-to-all(f32[128,1,128]{2,1,0:T(1,128)} %bitcast.42), channel_id=1, replica_groups=mesh['lon'=16,'ch'=8] {'lon','ch'}, dimensions={0} | all-to-all | bytes 131072 | tf_op jit(solution)/shard_map/all_to_all | solution.py:538
  172.5 0.2 reduce_sum.9
  172.6 0.6 subtract_add_fusion
  (6 shorter events, 0.1 us)
Async XLA Ops:
  0.6 40.4 %copy-start = (f32[1280,640]{1,0:T(8,128)S(1)}, f32[1280,640]{1,0:T(8,128)}, u32[]{:S(2)}) copy-start(f32[1280,640]{1,0:T(8,128)} %param.22) | copy-start | bytes 9830404
  6.6 22.7 %collective-permute-start.1 = (bf16[2,2,80,96]{3,2,1,0:T(8,128)(2,1)}, bf16[2,2,80,96]{3,2,1,0:T(8,128)(2,1)S(1)}, u32[]{:S(2)}, u32[]{:S(2)}) collective-permute-start(bf16[2,2,80,96]{3,2,1,0:T(8,128)(2,1)} %get-tuple-element.18), channel_id=1, source_target_pairs={{0,120},{8,0},{16,8},{24,16},{32,24},{40,32},{48,40},{56,48},{64,5... | collective-permute-start | bytes 184328 | tf_op jit(solution)/shard_map/ppermute | solution.py:575
  8.1 21.3 %collective-permute-start = (bf16[2,2,80,96]{3,2,1,0:T(8,128)(2,1)}, bf16[2,2,80,96]{3,2,1,0:T(8,128)(2,1)S(1)}, u32[]{:S(2)}, u32[]{:S(2)}) collective-permute-start(bf16[2,2,80,96]{3,2,1,0:T(8,128)(2,1)} %get-tuple-element.17), channel_id=1, source_target_pairs={{0,8},{8,16},{16,24},{24,32},{32,40},{40,48},{48,56},{56,64},{64,7... | collective-permute-start | bytes 184328 | tf_op jit(solution)/shard_map/ppermute | solution.py:574
  9.3 20.0 %all-to-all-start = ((f32[16,1,128]{2,1,0:T(1,128)}), f32[16,1,128]{2,1,0:T(1,128)S(1)}, u32[]{:S(2)}, u32[]{:S(2)}) async-start(f32[16,1,128]{2,1,0:T(1,128)} %bitcast.44), calls=%async_computation | async-start | bytes 16384 | tf_op jit(solution)/shard_map/all_to_all | solution.py:538
  29.4 0.6 copy-start.4
  29.4 0.6 copy-start.1
  29.4 0.6 copy-start.2
  32.3 5.4 %copy-start.8 = (s32[2]{0:T(128)S(1)}, s32[2]{0:T(128)}, u32[]{:S(2)}) copy-start(s32[2]{0:T(128)} %param.15) | copy-start | bytes 28
  32.3 5.4 %copy-start.9 = (s32[2]{0:T(128)S(1)}, s32[2]{0:T(128)}, u32[]{:S(2)}) copy-start(s32[2]{0:T(128)} %param.16) | copy-start | bytes 28
  32.3 6.4 %copy-start.7 = (f32[2,640]{1,0:T(2,128)S(1)}, f32[2,640]{1,0:T(2,128)}, u32[]{:S(2)}) copy-start(f32[2,640]{1,0:T(2,128)} %param.19) | copy-start | bytes 15364
  32.3 37.7 %all-to-all-start.1 = ((bf16[8,16,80,128]{3,2,1,0:T(8,128)(2,1)}), bf16[8,16,80,128]{3,2,1,0:T(8,128)(2,1)}, u32[]{:S(2)}, u32[]{:S(2)}) async-start(bf16[8,16,80,128]{3,2,1,0:T(8,128)(2,1)} %pack_halo.1), calls=%async_computation.1 | async-start | bytes 5242880 | tf_op jit(solution)/shard_map/all_to_all | solution.py:548
  37.6 5.1 %copy-start.5 = (f32[2,640]{1,0:T(2,128)S(1)}, f32[2,640]{1,0:T(2,128)}, u32[]{:S(2)}) copy-start(f32[2,640]{1,0:T(2,128)} %param.18) | copy-start | bytes 15364
  37.6 5.1 %copy-start.6 = (f32[2,640]{1,0:T(2,128)S(1)}, f32[2,640]{1,0:T(2,128)}, u32[]{:S(2)}) copy-start(f32[2,640]{1,0:T(2,128)} %param.20) | copy-start | bytes 15364
  96.9 33.8 %collective-permute-start.2 = (bf16[640,128]{1,0:T(8,128)(2,1)}, bf16[640,128]{1,0:T(8,128)(2,1)S(1)}, u32[]{:S(2)}, u32[]{:S(2)}) collective-permute-start(bf16[640,128]{1,0:T(8,128)(2,1)} %get-tuple-element.24), channel_id=1, source_target_pairs={{0,1},{1,2},{2,3},{3,4},{4,5},{5,6},{6,7},{8,9},{9,10},{10,11},{11... | collective-permute-start | bytes 491528 | tf_op jit(solution)/shard_map/ppermute | solution.py:600
  99.0 31.8 %collective-permute-start.3 = (bf16[640,128]{1,0:T(8,128)(2,1)}, bf16[640,128]{1,0:T(8,128)(2,1)}, u32[]{:S(2)}, u32[]{:S(2)}) collective-permute-start(bf16[640,128]{1,0:T(8,128)(2,1)} %get-tuple-element.25), channel_id=1, source_target_pairs={{1,0},{2,1},{3,2},{4,3},{5,4},{6,5},{7,6},{9,8},{10,9},{11,10},{12... | collective-permute-start | bytes 491528 | tf_op jit(solution)/shard_map/ppermute | solution.py:601
  100.3 30.5 %all-to-all-start.2 = ((f32[128,1,128]{2,1,0:T(1,128)}), f32[128,1,128]{2,1,0:T(1,128)S(1)}, u32[]{:S(2)}, u32[]{:S(2)}) async-start(f32[128,1,128]{2,1,0:T(1,128)} %bitcast.41), calls=%async_computation.2 | async-start | bytes 131072 | tf_op jit(solution)/shard_map/all_to_all | solution.py:538
  130.7 0.6 copy-start.3
  130.7 0.7 copy-start.10
